TPU v7x, 256 devices: a whole 4x4x8 slice. The times are simulated.
256 devices in a mesh: dp: 128 (over x, z, y), mp: 2 (over core).
Axes of the slice: x: 4, y: 4, z: 8, core: 2. Of those that a mesh axis runs over, the one named last changes fastest.
Arguments:
- queries: float32 [32768, 4096], P('dp', 'mp'), may hold values from -5 to 5
- passages: float32 [32768, 4096], P('dp', 'mp'), may hold values from -5 to 5
- cluster_of_block: int32 [128], replicated, may hold values from 0 to 63, never falling along the last dimension, each value on 1 to 4 neighbouring positions
- positive_row: int32 [32768], P('dp'), may hold values from 0 to 255
- query_weight: float32 [32768], P('dp'), may hold values from 0.3 to 3
Outputs:
- mean_loss: float32 [], replicated
- query_grad: float32 [32768, 4096], P('dp', 'mp')
- passage_grad: float32 [32768, 4096], P('dp', 'mp')
Inputs may be any that keep to these rules, and one draw needn't show every extreme that they name: `cluster_of_block`: never falls from one block to the next; every cluster covers 1 to 4 consecutive blocks, one exactly 4.
All inputs are finite; a program needn't handle non-finite values.
Results may differ from a plain program's by a relative error of at most 0.0051.
Values may be sent and summed in bfloat16 or wider, within the bound.
A program may use at most 128 MiB of HBM per device.

v0:
```python
import math

import jax
import jax.numpy as jnp
from jax import lax
from jax.sharding import PartitionSpec as P

CMAX = 4


def from_behind(block, axis, distance):
    devices = range(lax.axis_size(axis))
    route = [(i - distance, i) for i in devices if i - distance in devices]
    return lax.ppermute(block, axis, route)


def tile_dot(left_tile, right_tile):
    return lax.dot_general(
        left_tile, right_tile, (((1,), (1,)), ((), ())), preferred_element_type=jnp.float32
    )


def tile_back(coeff_tile, query_tile):
    return lax.dot_general(
        coeff_tile, query_tile, (((0,), (0,)), ((), ())), preferred_element_type=jnp.float32
    )


def shards(queries, passages, cluster_of_block, positive_row, query_weight):
    block_rows = queries.shape[0]
    half_width = queries.shape[1]
    score_scale = 3.0 / math.sqrt(half_width * lax.axis_size("mp"))
    my_index = lax.axis_index("dp")
    block_count = lax.axis_size("dp")
    query_half = queries.astype(jnp.bfloat16)
    passage_half = passages.astype(jnp.bfloat16)
    own_cluster = lax.dynamic_index_in_dim(cluster_of_block, my_index, 0, keepdims=False)
    offsets = [0]
    for distance in range(1, CMAX):
        offsets = offsets + [distance, -distance]
    zero_scores = jnp.zeros((block_rows, block_rows), jnp.float32)
    zero_rows = jnp.zeros((block_rows, half_width), jnp.float32)
    tiles = []
    flags = []
    partial_value = []
    for offset in offsets:
        if offset == 0:
            passage_tile = passage_half
        else:
            passage_tile = from_behind(passage_half, "dp", offset)
        source = my_index - offset
        inside = (source >= 0) & (source < block_count)
        clipped = jnp.clip(source, 0, block_count - 1)
        other_cluster = lax.dynamic_index_in_dim(cluster_of_block, clipped, 0, keepdims=False)
        linked_flag = inside & (other_cluster == own_cluster)
        partial_value.append(
            lax.cond(
                linked_flag,
                lambda other: tile_dot(query_half, other),
                lambda other: zero_scores,
                passage_tile,
            )
        )
        tiles.append(passage_tile)
        flags.append(linked_flag)
    scores = lax.psum(jnp.stack(partial_value), "mp")
    valid = jnp.stack(flags)
    masked = jnp.where(valid[:, None, None], scores * score_scale, -1e30)
    row_max = jnp.max(masked, axis=(0, 2))
    expo = jnp.exp(masked - row_max[None, :, None])
    row_total = jnp.sum(expo, axis=(0, 2))
    column_ids = jnp.arange(block_rows, dtype=jnp.int32)
    positive_hit = positive_row[:, None] == column_ids[None, :]
    picked = jnp.sum(jnp.where(positive_hit, masked[0], 0.0), axis=1)
    loss_rows = row_max + jnp.log(row_total) - picked
    loss_sum = lax.psum(jnp.sum(query_weight * loss_rows), "dp")
    mean_loss = loss_sum / (block_rows * block_count)
    weighted = query_weight[None, :, None] * (expo / row_total[None, :, None])
    own_term = weighted[0] - jnp.where(positive_hit, query_weight[:, None], 0.0)
    weighted = jnp.concatenate([own_term[None], weighted[1:]], 0)
    coeff = weighted.astype(jnp.bfloat16)
    query_grad = zero_rows
    for slot in range(len(offsets)):
        query_grad = query_grad + lax.cond(
            flags[slot],
            lambda coeff_tile, other: jnp.dot(
                coeff_tile, other, preferred_element_type=jnp.float32
            ),
            lambda coeff_tile, other: zero_rows,
            coeff[slot],
            tiles[slot],
        )
    passage_grad = tile_back(coeff[0], query_half)
    for slot in range(1, len(offsets)):
        offset = offsets[slot]
        grad_term = lax.cond(
            flags[slot],
            lambda coeff_tile: tile_back(coeff_tile, query_half),
            lambda coeff_tile: zero_rows,
            coeff[slot],
        )
        passage_grad = passage_grad + from_behind(grad_term, "dp", -offset)
    return (mean_loss, query_grad, passage_grad)


def solution(mesh):
    in_specs = (P("dp", "mp"), P("dp", "mp"), P(), P("dp"), P("dp"))
    out_specs = (P(), P("dp", "mp"), P("dp", "mp"))
    return jax.shard_map(shards, mesh=mesh, in_specs=in_specs, out_specs=out_specs, check_vma=False)
```

profile of v0, /device:TPU:0, one launch (start us, length us, event | category | flops | bytes accessed | tf_op | source)
XLA Modules:
  0.0 769.9 jit_solution(2785383667784089566)
XLA Ops:
  7.2 2.7 convert_element_type.20
  10.0 1.8 collective-permute-start
  11.8 1.3 collective-permute-start.1
  13.1 7.1 collective-permute-start.2
  20.2 1.3 collective-permute-start.3
  21.4 6.9 collective-permute-start.4
  28.3 7.2 collective-permute-done
  35.6 1.3 collective-permute-start.5
  39.0 1.7 convert_element_type.19
  48.8 1.7 conditional.20
  48.9 1.7 convolution_bitcast_fusion
  50.6 0.7 constant_dynamic-update-slice_fusion.6
  51.3 15.1 %collective-permute-done.1 = bf16[256,2048]{1,0:T(8,128)(2,1)} collective-permute-done((bf16[256,2048]{1,0:T(8,128)(2,1)}, bf16[256,2048]{1,0:T(8,128)(2,1)}, u32[]{:S(2)}, u32[]{:S(2)}) %collective-permute-start.1) | collective-permute-done | bytes 1048608 | tf_op jit(solution)/shard_map/ppermute | solution.py:14
  66.4 1.7 conditional.22
  66.4 1.7 convolution_bitcast_fusion.2
  68.2 3.4 collective-permute-done.3
  71.6 2.5 conditional.24
  71.6 2.5 convolution_bitcast_fusion.4
  74.2 33.2 %collective-permute-done.4 = bf16[256,2048]{1,0:T(8,128)(2,1)} collective-permute-done((bf16[256,2048]{1,0:T(8,128)(2,1)}, bf16[256,2048]{1,0:T(8,128)(2,1)}, u32[]{:S(2)}, u32[]{:S(2)}) %collective-permute-start.4) | collective-permute-done | bytes 1048608 | tf_op jit(solution)/shard_map/ppermute | solution.py:14
  108.1 1.0 constant_dynamic-update-slice_fusion.3
  109.2 1.0 constant_dynamic-update-slice_fusion.2
  110.2 1.7 conditional.26
  110.2 1.7 convolution_bitcast_fusion.6
  111.9 1.2 copy-done.2
  113.3 45.6 %all-reduce.2.cloned.1.call-done = f32[7,256,256]{2,1,0:T(8,128)} async-done(((f32[7,256,256]{2,1,0:T(8,128)}), f32[7,256,256]{2,1,0:T(8,128)}) %all-reduce.2.cloned.1.call-update) | async-done | bytes 1835024 | tf_op jit(solution)/shard_map/psum | solution.py:66
  158.9 1.8 fusion.11
  161.2 1.7 fusion.10
  163.6 2.8 conditional.39
  163.6 2.8 fusion.25
  166.4 4.5 collective-permute-start.11
  170.9 1.6 conditional.38
  170.9 1.6 broadcast_in_dim.75
  172.4 1.3 collective-permute-start.10
  173.7 1.9 conditional.37
  173.7 1.9 fusion.23
  175.6 4.8 collective-permute-start.9
  180.5 1.6 conditional.36
  180.5 1.6 broadcast_in_dim.64
  182.0 1.3 collective-permute-start.8
  183.3 1.9 conditional.35
  183.3 1.9 fusion.21
  185.2 6.1 collective-permute-start.7
  191.3 1.6 conditional.34
  191.3 1.6 broadcast_in_dim.60
  192.9 112.1 %collective-permute-done.11 = f32[256,2048]{1,0:T(8,128)} collective-permute-done((f32[256,2048]{1,0:T(8,128)}, f32[256,2048]{1,0:T(8,128)}, u32[]{:S(2)}, u32[]{:S(2)}) %collective-permute-start.11) | collective-permute-done | bytes 2097184 | tf_op jit(solution)/shard_map/ppermute | solution.py:14
  305.1 1.3 collective-permute-start.6
  307.2 423.1 %psum.15 = f32[]{:T(128)} all-reduce(f32[]{:T(128)} %multiply_reduce_fusion), channel_id=1, replica_groups=mesh['dp'=128,'mp'=2] {'dp'}, use_global_device_ids=true, to_apply=%region_19.20 | all-reduce | flops 1 | bytes 8 | tf_op jit(solution)/shard_map/psum | solution.py:76
  730.2 1.1 fusion.9
  732.0 1.8 conditional.33
  732.0 1.7 fusion.19
  733.7 1.6 conditional.32
  733.7 1.6 broadcast_in_dim.56
  735.3 3.1 conditional.31
  735.3 3.1 fusion.17
  738.4 1.6 conditional.30
  738.4 1.6 broadcast_in_dim.52
  740.0 3.0 conditional.29
  740.0 3.0 fusion.15
  743.0 3.0 conditional.27
  743.0 3.0 fusion.13
  745.9 1.6 conditional.28
  745.9 1.6 broadcast_in_dim.48
  747.5 7.6 add_add_fusion
  755.1 6.8 fusion.4
  (46 shorter events, 4.4 us)
Async XLA Ops:
  7.2 29.7 %copy-start.8 = (s32[128]{0:T(128)S(1)}, s32[128]{0:T(128)}, u32[]{:S(2)}) copy-start(s32[128]{0:T(128)} %param.47) | copy-start | bytes 1540
  7.2 151.7 %all-reduce.2.cloned.1.call-start = ((), (), s32[]{:S(2)}) async-start(), calls=%async_computation | async-start | bytes 3670016 | tf_op jit(solution)/shard_map/psum | solution.py:66
  10.0 25.6 %collective-permute-start = (bf16[256,2048]{1,0:T(8,128)(2,1)}, bf16[256,2048]{1,0:T(8,128)(2,1)S(1)}, u32[]{:S(2)}, u32[]{:S(2)}) collective-permute-start(bf16[256,2048]{1,0:T(8,128)(2,1)} %convert_element_type.20), channel_id=1, source_target_pairs={{0,2},{2,4},{4,6},{6,8},{8,10},{10,12},{12,14},{14,16},{16,18},{18... | collective-permute-start | bytes 3145736 | tf_op jit(solution)/shard_map/ppermute | solution.py:14
  11.8 54.7 %collective-permute-start.1 = (bf16[256,2048]{1,0:T(8,128)(2,1)}, bf16[256,2048]{1,0:T(8,128)(2,1)}, u32[]{:S(2)}, u32[]{:S(2)}) collective-permute-start(bf16[256,2048]{1,0:T(8,128)(2,1)} %convert_element_type.20), channel_id=1, source_target_pairs={{2,0},{4,2},{6,4},{8,6},{10,8},{12,10},{14,12},{16,14},{18,16},{20... | collective-permute-start | bytes 3145736 | tf_op jit(solution)/shard_map/ppermute | solution.py:14
  13.1 55.1 %collective-permute-start.2 = (bf16[256,2048]{1,0:T(8,128)(2,1)}, bf16[256,2048]{1,0:T(8,128)(2,1)}, u32[]{:S(2)}, u32[]{:S(2)}) collective-permute-start(bf16[256,2048]{1,0:T(8,128)(2,1)} %convert_element_type.20), channel_id=1, source_target_pairs={{0,4},{2,6},{4,8},{6,10},{8,12},{10,14},{12,16},{14,18},{16,20},{1... | collective-permute-start | bytes 3145736 | tf_op jit(solution)/shard_map/ppermute | solution.py:14
  20.2 51.5 %collective-permute-start.3 = (bf16[256,2048]{1,0:T(8,128)(2,1)}, bf16[256,2048]{1,0:T(8,128)(2,1)}, u32[]{:S(2)}, u32[]{:S(2)}) collective-permute-start(bf16[256,2048]{1,0:T(8,128)(2,1)} %convert_element_type.20), channel_id=1, source_target_pairs={{4,0},{6,2},{8,4},{10,6},{12,8},{14,10},{16,12},{18,14},{20,16},{2... | collective-permute-start | bytes 3145736 | tf_op jit(solution)/shard_map/ppermute | solution.py:14
  21.4 85.9 %collective-permute-start.4 = (bf16[256,2048]{1,0:T(8,128)(2,1)}, bf16[256,2048]{1,0:T(8,128)(2,1)}, u32[]{:S(2)}, u32[]{:S(2)}) collective-permute-start(bf16[256,2048]{1,0:T(8,128)(2,1)} %convert_element_type.20), channel_id=1, source_target_pairs={{0,6},{2,8},{4,10},{6,12},{8,14},{10,16},{12,18},{14,20},{16,22},{... | collective-permute-start | bytes 3145736 | tf_op jit(solution)/shard_map/ppermute | solution.py:14
  35.6 15.7 %copy-start = (bf16[256,2048]{1,0:T(8,128)(2,1)}, bf16[256,2048]{1,0:T(8,128)(2,1)S(1)}, u32[]{:S(2)}) copy-start(bf16[256,2048]{1,0:T(8,128)(2,1)S(1)} %collective-permute-done) | copy-start | bytes 3145732
  35.6 74.6 %collective-permute-start.5 = (bf16[256,2048]{1,0:T(8,128)(2,1)}, bf16[256,2048]{1,0:T(8,128)(2,1)}, u32[]{:S(2)}, u32[]{:S(2)}) collective-permute-start(bf16[256,2048]{1,0:T(8,128)(2,1)} %convert_element_type.20), channel_id=1, source_target_pairs={{6,0},{8,2},{10,4},{12,6},{14,8},{16,10},{18,12},{20,14},{22,16},{... | collective-permute-start | bytes 3145736 | tf_op jit(solution)/shard_map/ppermute | solution.py:14
  68.2 3.4 copy-start.6
  71.6 36.5 %copy-start.1 = (f32[7,256,256]{2,1,0:T(8,128)S(1)}, f32[7,256,256]{2,1,0:T(8,128)}, u32[]{:S(2)}) copy-start(f32[7,256,256]{2,1,0:T(8,128)} %constant_dynamic-update-slice_fusion.6) | copy-start | bytes 5505028
  108.1 2.0 copy-start.7
  111.9 1.2 copy-start.2
  113.3 47.9 %copy-start.9 = (f32[256]{0:T(256)S(1)}, f32[256]{0:T(256)}, u32[]{:S(2)}) copy-start(f32[256]{0:T(256)} %param.49) | copy-start | bytes 3076
  163.6 7.3 copy-start.5
  163.6 10.1 %copy-start.4 = (bf16[256,256]{1,0:T(8,128)(2,1)}, bf16[256,256]{1,0:T(8,128)(2,1)S(1)}, u32[]{:S(2)}) copy-start(bf16[256,256]{1,0:T(8,128)(2,1)S(1)} %get-tuple-element.197) | copy-start | bytes 393220
  163.6 16.9 %copy-start.3 = (bf16[256,256]{1,0:T(8,128)(2,1)}, bf16[256,256]{1,0:T(8,128)(2,1)S(1)}, u32[]{:S(2)}) copy-start(bf16[256,256]{1,0:T(8,128)(2,1)S(1)} %get-tuple-element.198) | copy-start | bytes 393220
  166.4 138.6 %collective-permute-start.11 = (f32[256,2048]{1,0:T(8,128)}, f32[256,2048]{1,0:T(8,128)}, u32[]{:S(2)}, u32[]{:S(2)}) collective-permute-start(f32[256,2048]{1,0:T(8,128)} %get-tuple-element.227), channel_id=1, source_target_pairs={{0,6},{2,8},{4,10},{6,12},{8,14},{10,16},{12,18},{14,20},{16,22},{... | collective-permute-start | bytes 6291464 | tf_op jit(solution)/shard_map/ppermute | solution.py:14
  172.4 582.6 %collective-permute-start.10 = (f32[256,2048]{1,0:T(8,128)}, f32[256,2048]{1,0:T(8,128)}, u32[]{:S(2)}, u32[]{:S(2)}) collective-permute-start(f32[256,2048]{1,0:T(8,128)} %get-tuple-element.226), channel_id=1, source_target_pairs={{6,0},{8,2},{10,4},{12,6},{14,8},{16,10},{18,12},{20,14},{22,16},{... | collective-permute-start | bytes 6291464 | tf_op jit(solution)/shard_map/ppermute | solution.py:14
  175.6 579.5 %collective-permute-start.9 = (f32[256,2048]{1,0:T(8,128)}, f32[256,2048]{1,0:T(8,128)}, u32[]{:S(2)}, u32[]{:S(2)}) collective-permute-start(f32[256,2048]{1,0:T(8,128)} %get-tuple-element.225), channel_id=1, source_target_pairs={{0,4},{2,6},{4,8},{6,10},{8,12},{10,14},{12,16},{14,18},{16,20},{1... | collective-permute-start | bytes 6291464 | tf_op jit(solution)/shard_map/ppermute | solution.py:14
  182.0 573.0 %collective-permute-start.8 = (f32[256,2048]{1,0:T(8,128)}, f32[256,2048]{1,0:T(8,128)}, u32[]{:S(2)}, u32[]{:S(2)}) collective-permute-start(f32[256,2048]{1,0:T(8,128)} %get-tuple-element.224), channel_id=1, source_target_pairs={{4,0},{6,2},{8,4},{10,6},{12,8},{14,10},{16,12},{18,14},{20,16},{2... | collective-permute-start | bytes 6291464 | tf_op jit(solution)/shard_map/ppermute | solution.py:14
  185.2 569.9 %collective-permute-start.7 = (f32[256,2048]{1,0:T(8,128)}, f32[256,2048]{1,0:T(8,128)}, u32[]{:S(2)}, u32[]{:S(2)}) collective-permute-start(f32[256,2048]{1,0:T(8,128)} %get-tuple-element.223), channel_id=1, source_target_pairs={{0,2},{2,4},{4,6},{6,8},{8,10},{10,12},{12,14},{14,16},{16,18},{18... | collective-permute-start | bytes 6291464 | tf_op jit(solution)/shard_map/ppermute | solution.py:14
  191.3 115.0 %copy-start.10 = (s32[256]{0:T(256)S(1)}, s32[256]{0:T(256)}, u32[]{:S(2)}) copy-start(s32[256]{0:T(256)} %param.48) | copy-start | bytes 3076
  305.1 450.0 %collective-permute-start.6 = (f32[256,2048]{1,0:T(8,128)}, f32[256,2048]{1,0:T(8,128)}, u32[]{:S(2)}, u32[]{:S(2)}) collective-permute-start(f32[256,2048]{1,0:T(8,128)} %get-tuple-element.222), channel_id=1, source_target_pairs={{2,0},{4,2},{6,4},{8,6},{10,8},{12,10},{14,12},{16,14},{18,16},{20... | collective-permute-start | bytes 6291464 | tf_op jit(solution)/shard_map/ppermute | solution.py:14
Sparse Core Ops, SparseCore 0:
  113.3 45.5 all-reduce.1
where the time goes:
time: 769 us; the launch traced here: 770 us
  blocking collectives  423 us (55%)
  waiting for transfers between devices  217 us (28%)
  starting transfers between devices  38.9 us (5%)
  matrix products  31.8 us (4%)
  between operations  25.6 us (3%)
  other arithmetic  17.9 us (2%)
  local copies, waits for them, and re-layouts  15.7 us (2%)
    psum x1, blocking collectives, shards(): loss_sum = lax.psum(jnp.sum(query_weight * loss_rows), 'dp')  423 us
    ppermute x12, waiting for transfers between devices, from_behind(): return lax.ppermute(block, axis, route)  171 us
    psum x1, waiting for transfers between devices, shards(): scores = lax.psum(jnp.stack(partial_value), 'mp')  45.6 us
    ppermute x12, starting transfers between devices, from_behind(): return lax.ppermute(block, axis, route)  38.9 us
  transfers between devices with their start and end apart: 13, of which 6 were waited for; matrix products, arithmetic and copies ran while one was open for 6% of the time, Pallas kernels for 0%

commit v1 on v0

v1 whole, which is shorter than its diff:
```python
import functools
import math

import jax
import jax.numpy as jnp
from jax import lax
from jax.experimental import pallas as pl
from jax.experimental.pallas import tpu as pltpu
from jax.sharding import PartitionSpec as P

MESH = pl.DeviceIdType.MESH
NY, NZ, NX = 4, 8, 4
CHUNK = 256
GROUP = 32


def nt_dot(left, right):
    return lax.dot_general(left, right, (((1,), (1,)), ((), ())), preferred_element_type=jnp.float32)


def nn_dot(left, right):
    return jnp.dot(left, right, preferred_element_type=jnp.float32)


def kernel(
    query_hbm, passage_hbm, cluster, positive, weight,
    loss_ref, query_grad_hbm, passage_grad_hbm,
    fresh, own, beside, staged, gathered,
    score_own, score_other, coeff, coeff_out, coeff_beside, coeff_staged, coeff_got, coeff_fwd, coeff_t,
    pos_cols, weight_cols, query_grad, passage_grad, loss_tile, loss_y, loss_z, loss_x,
    in_sem, z_send, z_recv, y_send, y_recv, s_send, s_recv,
    cz_send, cz_recv, cy_send, cy_recv, cf_send, cf_recv,
    ly_send, ly_recv, lz_send, lz_recv, lx_send, lx_recv, qg_sem, pg_sem,
):
    rows, width = query_hbm.shape
    count = width // CHUNK
    half = rows // 2
    planes = NX * NZ
    me = lax.axis_index("dp")
    core = lax.axis_index("mp")
    y = me % NY
    plane = me // NY
    z = plane % NZ
    x = plane // NZ

    def at_y(step):
        return plane * NY + (y + step) % NY

    def at_z(step):
        return (x * NZ + (z + step) % NZ) * NY + y

    def at_x(step):
        return (((x + step) % NX) * NZ + z) * NY + y

    left_plane = ((plane + planes - 1) % planes) * NY + y
    right_plane = ((plane + 1) % planes) * NY + y

    def arriving(k):
        start = pl.multiple_of(k * CHUNK, CHUNK)
        return pltpu.make_async_copy(passage_hbm.at[:, pl.ds(start, CHUNK)], fresh.at[k], in_sem.at[k])

    def arriving_query(k):
        start = pl.multiple_of(k * CHUNK, CHUNK)
        return pltpu.make_async_copy(
            query_hbm.at[:, pl.ds(start, CHUNK)], fresh.at[count + k], in_sem.at[count + k]
        )

    def start_in(k, carry):
        arriving(k).start()
        return carry

    def start_in_query(k, carry):
        arriving_query(k).start()
        return carry

    lax.fori_loop(0, count, start_in, 0)
    lax.fori_loop(0, count, start_in_query, 0)

    barrier = pltpu.get_barrier_semaphore()
    peers = [at_y(s) for s in range(1, NY)] + [at_z(s) for s in range(1, NZ)] + [at_x(s) for s in range(1, NX)]
    peers = peers + [left_plane, right_plane]
    for peer in peers:
        pl.semaphore_signal(barrier, inc=1, device_id=(peer, core), device_id_type=MESH)
    pl.semaphore_signal(barrier, inc=1, device_id=(me, 1 - core), device_id_type=MESH)
    pl.semaphore_wait(barrier, len(peers) + 1)

    last = planes * NY - 1
    mine = cluster[me]
    on_left = cluster[jnp.maximum(me - NY, 0)]
    on_right = cluster[jnp.minimum(me + NY, last)]
    has_left = plane > 0
    has_right = plane < planes - 1
    want_left, want_right, linked = [], [], [None]
    for step in range(1, NY):
        target = at_y(step)
        theirs = cluster[target]
        want_left.append(has_left & (theirs == on_left))
        want_right.append(has_right & (theirs == on_right))
        near = theirs == mine
        near = near | (has_left & (cluster[jnp.maximum(target - NY, 0)] == mine))
        near = near | (has_right & (cluster[jnp.minimum(target + NY, last)] == mine))
        linked.append(near)

    def pick(step, here, from_left, from_right):
        return lax.select(
            want_left[step - 1], from_left, lax.select(want_right[step - 1], from_right, here)
        )

    def send(source, target, send_sem, recv_sem, place, where=None):
        return pltpu.make_async_remote_copy(
            src_ref=source, dst_ref=target, send_sem=send_sem, recv_sem=recv_sem,
            device_id=(place, core if where is None else where), device_id_type=MESH,
        )

    def along_z(k):
        return [
            send(own.at[k], beside.at[0, k], z_send.at[0, k], z_recv.at[0, k], right_plane),
            send(own.at[k], beside.at[1, k], z_send.at[1, k], z_recv.at[1, k], left_plane),
        ]

    def along_y(k):
        return [
            send(
                staged.at[s - 1, k], gathered.at[NY - s - 1, k],
                y_send.at[s - 1, k], y_recv.at[NY - s - 1, k], at_y(s),
            )
            for s in range(1, NY)
        ]

    def share(k):
        for copy in along_z(k):
            copy.start()

    def relay(k):
        for copy in along_z(k):
            copy.wait_recv()
        here, from_left, from_right = own[k], beside[0, k], beside[1, k]
        for s in range(1, NY):
            staged[s - 1, k] = pick(s, here, from_left, from_right)
        for copy in along_y(k):
            copy.start()

    def landed(k):
        for copy in along_y(k):
            copy.wait_recv()

    def block(k, slot):
        return own[k] if slot == 0 else gathered[slot - 1, k]

    def add_scores(k, first=False):
        mine_now = own[count + k]
        for slot in range(NY):
            columns = slice(slot * rows, (slot + 1) * rows)
            part = nt_dot(mine_now, block(k, slot))
            if first:
                score_own[:, columns] = part
            else:
                score_own[:, columns] += part

    def cast_passage(k):
        arriving(k).wait()
        own[k] = fresh[k].astype(jnp.bfloat16)

    for k in range(3):
        cast_passage(k)
        share(k)

    def cast_rest(k, carry):
        cast_passage(k)
        return carry

    def cast_queries(k, carry):
        arriving_query(k).wait()
        own[count + k] = fresh[count + k].astype(jnp.bfloat16)
        return carry

    lax.fori_loop(3, count, cast_rest, 0)
    lax.fori_loop(0, count, cast_queries, 0)

    for part in range(rows // 128):
        here = slice(part * 128, (part + 1) * 128)
        as_row = positive[part : part + 1, :].astype(jnp.float32)
        pos_cols[here, :] = jnp.broadcast_to(as_row, (128, 128)).T
        weight_cols[here, :] = jnp.broadcast_to(weight[part : part + 1, :], (128, 128)).T

    relay(0)
    share(3)
    relay(1)
    share(4)
    landed(0)
    add_scores(0, first=True)

    def passage_step(k, carry):
        relay(k)
        share(k + 3)
        landed(k - 1)
        add_scores(k - 1)
        return carry

    lax.fori_loop(2, count, passage_step, 0)
    relay(count)
    share(count + 3)
    landed(count - 1)
    add_scores(count - 1)
    swap = send(score_own, score_other, s_send, s_recv, me, 1 - core)
    swap.start()
    relay(count + 1)
    share(count + 4)
    swap.wait_recv()

    scale = 3.0 / math.sqrt(2 * width)

    def soft_rows(group, total):
        here = pl.ds(pl.multiple_of(group * GROUP, GROUP), GROUP)
        tiles = []
        for slot in range(NY):
            columns = slice(slot * rows, (slot + 1) * rows)
            tile = (score_own[here, columns] + score_other[here, columns]) * scale
            if slot > 0:
                tile = lax.select(linked[slot], tile, jnp.full_like(tile, -1e30))
            tiles.append(tile)
        top = functools.reduce(jnp.maximum, [jnp.max(t, axis=1, keepdims=True) for t in tiles])
        expo = [jnp.exp(t - top) for t in tiles]
        row_total = functools.reduce(jnp.add, [jnp.sum(e, axis=1, keepdims=True) for e in expo])
        wanted = pos_cols[here, 0:1]
        heavy = weight_cols[here, 0:1]
        columns = lax.broadcasted_iota(jnp.int32, (GROUP, rows), 1).astype(jnp.float32)
        hit = columns == wanted
        picked = jnp.sum(jnp.where(hit, tiles[0], 0.0), axis=1, keepdims=True)
        ratio = heavy / row_total
        for slot in range(NY):
            value = expo[slot] * ratio
            if slot == 0:
                value = value - jnp.where(hit, heavy, 0.0)
            coeff[slot, here, :] = value.astype(jnp.bfloat16)
        return total + heavy * (top + jnp.log(row_total) - picked)

    total = lax.fori_loop(0, rows // GROUP, soft_rows, jnp.zeros((GROUP, 1), jnp.float32))
    loss_tile[...] = jnp.broadcast_to(jnp.sum(total, axis=0, keepdims=True), loss_tile.shape)

    my_half = pl.ds(pl.multiple_of(core * half, half), half)
    for s in range(1, NY):
        coeff_out[s - 1] = coeff[s, my_half, :]
    coeff_z = [
        send(coeff_out, coeff_beside.at[0], cz_send.at[0], cz_recv.at[0], right_plane),
        send(coeff_out, coeff_beside.at[1], cz_send.at[1], cz_recv.at[1], left_plane),
    ]
    for copy in coeff_z:
        copy.start()

    def spread(buffer, send_sem, recv_sem, mine_at, size, place):
        return [
            send(loss_tile, buffer.at[mine_at], send_sem.at[s - 1], recv_sem.at[mine_at], place(s))
            for s in range(1, size)
        ]

    def collect(buffer, recv_sem, mine_at, size):
        buffer[mine_at] = loss_tile[...]
        for s in range(1, size):
            source = (mine_at + s) % size
            send(loss_tile, buffer.at[source], recv_sem.at[source], recv_sem.at[source], me, 1 - core).wait_recv()
        value = buffer[0]
        for s in range(1, size):
            value = value + buffer[s]
        return value

    loss_along_y = spread(loss_y, ly_send, ly_recv, y, NY, at_y)
    for copy in loss_along_y:
        copy.start()

    landed(count)
    relay(count + 2)
    share(count + 5)

    def query_grad_step(k, carry):
        value = nn_dot(coeff[0], own[k])
        for slot in range(1, NY):
            value = value + nn_dot(coeff[slot], gathered[slot - 1, k])
        query_grad[k] = value
        start = pl.multiple_of(k * CHUNK, CHUNK)
        pltpu.make_async_copy(query_grad.at[k], query_grad_hbm.at[:, pl.ds(start, CHUNK)], qg_sem.at[k]).start()
        return carry

    lax.fori_loop(0, count, query_grad_step, 0)

    for copy in coeff_z:
        copy.wait_recv()
    for s in range(1, NY):
        coeff_staged[s - 1] = pick(s, coeff_out[s - 1], coeff_beside[0, s - 1], coeff_beside[1, s - 1])
    coeff_y = [
        send(
            coeff_staged.at[s - 1], coeff_got.at[NY - s - 1], cy_send.at[s - 1], cy_recv.at[NY - s - 1], at_y(s)
        )
        for s in range(1, NY)
    ]
    for copy in coeff_y:
        copy.start()

    landed(count + 1)
    relay(count + 3)
    share(count + 6)
    value = collect(loss_y, ly_recv, y, NY)
    for copy in loss_along_y:
        copy.wait_send()
    loss_tile[...] = value
    loss_along_z = spread(loss_z, lz_send, lz_recv, z, NZ, at_z)
    for copy in loss_along_z:
        copy.start()

    landed(count + 2)
    relay(count + 4)
    share(count + 7)
    for copy in coeff_y:
        copy.wait_recv()
    forward = send(coeff_got, coeff_fwd, cf_send, cf_recv, me, 1 - core)
    forward.start()
    value = collect(loss_z, lz_recv, z, NZ)
    for copy in loss_along_z:
        copy.wait_send()
    loss_tile[...] = value
    loss_along_x = spread(loss_x, lx_send, lx_recv, x, NX, at_x)
    for copy in loss_along_x:
        copy.start()

    landed(count + 3)
    relay(count + 5)
    forward.wait_recv()

    coeff_t[0] = coeff[0].astype(jnp.float32).T.astype(jnp.bfloat16)
    first_half = core == 0
    for slot in range(1, NY):
        got, fwd = coeff_got[slot - 1], coeff_fwd[slot - 1]
        tile = jnp.concatenate([lax.select(first_half, got, fwd), lax.select(first_half, fwd, got)], axis=0)
        tile = tile.astype(jnp.float32).T
        tile = lax.select(linked[slot], tile, jnp.zeros_like(tile))
        coeff_t[slot] = tile.astype(jnp.bfloat16)

    landed(count + 4)
    relay(count + 6)
    value = collect(loss_x, lx_recv, x, NX)
    for copy in loss_along_x:
        copy.wait_send()
    loss_ref[...] = value * (1.0 / (rows * planes * NY))

    def passage_grad_out(k):
        start = pl.multiple_of(k * CHUNK, CHUNK)
        return pltpu.make_async_copy(
            passage_grad.at[k], passage_grad_hbm.at[:, pl.ds(start, CHUNK)], pg_sem.at[k]
        )

    def passage_grad_step(k, carry):
        value = nn_dot(coeff_t[0], own[count + k])
        for slot in range(1, NY):
            value = value + nn_dot(coeff_t[slot], gathered[slot - 1, count + k])
        passage_grad[k] = value
        passage_grad_out(k).start()
        return carry

    landed(count + 5)
    relay(count + 7)
    lax.fori_loop(0, 6, passage_grad_step, 0)
    landed(count + 6)
    passage_grad_step(6, 0)
    landed(count + 7)
    passage_grad_step(7, 0)

    def finish_sends(k, carry):
        for copy in along_z(k):
            copy.wait_send()
        for copy in along_y(k):
            copy.wait_send()
        return carry

    lax.fori_loop(0, 2 * count, finish_sends, 0)
    for copy in coeff_z + coeff_y + [swap, forward]:
        copy.wait_send()

    def finish_out(k, carry):
        start = pl.multiple_of(k * CHUNK, CHUNK)
        pltpu.make_async_copy(query_grad.at[k], query_grad_hbm.at[:, pl.ds(start, CHUNK)], qg_sem.at[k]).wait()
        passage_grad_out(k).wait()
        return carry

    lax.fori_loop(0, count, finish_out, 0)


def shards(queries, passages, cluster_of_block, positive_row, query_weight):
    rows, width = queries.shape
    count = width // CHUNK
    dma = pltpu.SemaphoreType.DMA
    vmem = pltpu.VMEM
    low, full = jnp.bfloat16, jnp.float32
    tile = (8, 128)
    scratch = [
        vmem((2 * count, rows, CHUNK), full),
        vmem((2 * count, rows, CHUNK), low),
        vmem((2, 2 * count, rows, CHUNK), low),
        vmem((NY - 1, 2 * count, rows, CHUNK), low),
        vmem((NY - 1, 2 * count, rows, CHUNK), low),
        vmem((rows, NY * rows), full),
        vmem((rows, NY * rows), full),
        vmem((NY, rows, rows), low),
        vmem((NY - 1, rows // 2, rows), low),
        vmem((2, NY - 1, rows // 2, rows), low),
        vmem((NY - 1, rows // 2, rows), low),
        vmem((NY - 1, rows // 2, rows), low),
        vmem((NY - 1, rows // 2, rows), low),
        vmem((NY, rows, rows), low),
        vmem((rows, 128), full),
        vmem((rows, 128), full),
        vmem((count, rows, CHUNK), full),
        vmem((count, rows, CHUNK), full),
        vmem(tile, full),
        vmem((NY,) + tile, full),
        vmem((NZ,) + tile, full),
        vmem((NX,) + tile, full),
        dma((2 * count,)),
        dma((2, 2 * count)),
        dma((2, 2 * count)),
        dma((NY - 1, 2 * count)),
        dma((NY - 1, 2 * count)),
        dma, dma,
        dma((2,)), dma((2,)),
        dma((NY - 1,)), dma((NY - 1,)),
        dma, dma,
        dma((NY,)), dma((NY,)),
        dma((NZ,)), dma((NZ,)),
        dma((NX,)), dma((NX,)),
        dma((count,)), dma((count,)),
    ]
    anywhere = pl.BlockSpec(memory_space=pl.ANY)
    in_vmem = pl.BlockSpec(memory_space=pltpu.VMEM)
    loss, query_grad, passage_grad = pl.pallas_call(
        kernel,
        out_shape=[
            jax.ShapeDtypeStruct(tile, full),
            jax.ShapeDtypeStruct((rows, width), full),
            jax.ShapeDtypeStruct((rows, width), full),
        ],
        in_specs=[anywhere, anywhere, pl.BlockSpec(memory_space=pltpu.SMEM), in_vmem, in_vmem],
        out_specs=[in_vmem, anywhere, anywhere],
        scratch_shapes=scratch,
        compiler_params=pltpu.CompilerParams(
            collective_id=0, has_side_effects=True, vmem_limit_bytes=56 * 2**20
        ),
        cost_estimate=pl.CostEstimate(
            flops=6 * NY * rows * rows * width, bytes_accessed=16 * rows * width, transcendentals=NY * rows * rows
        ),
    )(
        queries, passages, cluster_of_block,
        positive_row.reshape(rows // 128, 128), query_weight.reshape(rows // 128, 128),
    )
    return loss[0, 0], query_grad, passage_grad


def solution(mesh):
    in_specs = (P("dp", "mp"), P("dp", "mp"), P(), P("dp"), P("dp"))
    out_specs = (P(), P("dp", "mp"), P("dp", "mp"))
    return jax.shard_map(shards, mesh=mesh, in_specs=in_specs, out_specs=out_specs, check_vma=False)
```

time: 769 us -> 122 us (0.16)
  the two profiles are of different devices: /device:TPU:0 before, /device:TPU:1 now
where the time goes in v1:
time: 122 us
  Pallas kernels  115 us (94%)
  local copies, waits for them, and re-layouts  5.79 us (5%)
    pallas_call x1, Pallas kernels, shards(): pl.pallas_call(kernel, out_shape=[jax.ShapeDtypeStruct(tile, full), jax.S...  115 us
    unnamed x4, local copies, waits for them, and re-layouts  4.61 us

profile of v1, /device:TPU:1, one launch (start us, length us, event | category | flops | bytes accessed | tf_op | source)
XLA Modules:
  0.0 121.7 jit_solution(283618575978912711)
XLA Ops:
  0.6 115.3 %shard_map.76 = (f32[8,128]{1,0:T(8,128)}, f32[256,2048]{1,0:T(8,128)}, f32[256,2048]{1,0:T(8,128)}) custom-call(f32[256,2048]{1,0:T(8,128)} %query_hbm.1, f32[256,2048]{1,0:T(8,128)} %passage_hbm.1, s32[128]{0:T(128)} %cluster.1, s32[2,128]{1,0:T(2,128)} %bitcast.3, f32[2,128]{1,0:T(2,128)} %bitcast.4), custom_call_target="tpu_custom_call" | custom-call | flops 3221225472 | bytes 8388608 | tf_op jit(solution)/shard_map/pallas_call | solution.py:433
  115.9 1.2 slice.3
  117.1 0.0 copy-start
  117.1 3.3 %copy.10 = f32[256,2048]{1,0:T(8,128)} copy(f32[256,2048]{1,0:T(8,128)} %get-tuple-element.13) | data formatting | bytes 4194304
  120.4 0.0 copy-done
  120.4 1.3 %copy.11 = f32[256,2048]{1,0:T(8,128)} copy(f32[256,2048]{1,0:T(8,128)S(1)} %copy-done) | data formatting | bytes 4194304
Async XLA Ops:
  117.1 3.3 %copy-start = (f32[256,2048]{1,0:T(8,128)S(1)}, f32[256,2048]{1,0:T(8,128)}, u32[]{:S(2)}) copy-start(f32[256,2048]{1,0:T(8,128)} %get-tuple-element.14) | copy-start | bytes 6291460

commit v2 on v1

--- a/solution.py
+++ b/solution.py
@@ -24,13 +24,13 @@
 
 def kernel(
     query_hbm, passage_hbm, cluster, positive, weight,
-    loss_ref, query_grad_hbm, passage_grad_hbm,
-    fresh, own, beside, staged, gathered,
+    loss_ref, query_grad, passage_grad,
+    fresh, own, beside, staged, gathered, raw, raw_beside,
     score_own, score_other, coeff, coeff_out, coeff_beside, coeff_staged, coeff_got, coeff_fwd, coeff_t,
-    pos_cols, weight_cols, query_grad, passage_grad, loss_tile, loss_y, loss_z, loss_x,
+    pos_cols, weight_cols, loss_tile, loss_y, loss_z, loss_x,
     in_sem, z_send, z_recv, y_send, y_recv, s_send, s_recv,
     cz_send, cz_recv, cy_send, cy_recv, cf_send, cf_recv,
-    ly_send, ly_recv, lz_send, lz_recv, lx_send, lx_recv, qg_sem, pg_sem,
+    ly_send, ly_recv, lz_send, lz_recv, lx_send, lx_recv, raw_send, raw_recv,
 ):
     rows, width = query_hbm.shape
     count = width // CHUNK
@@ -91,15 +91,18 @@
     has_left = plane > 0
     has_right = plane < planes - 1
     want_left, want_right, linked = [], [], [None]
+    got_left, got_right = [None], [None]
     for step in range(1, NY):
         target = at_y(step)
         theirs = cluster[target]
         want_left.append(has_left & (theirs == on_left))
         want_right.append(has_right & (theirs == on_right))
-        near = theirs == mine
-        near = near | (has_left & (cluster[jnp.maximum(target - NY, 0)] == mine))
-        near = near | (has_right & (cluster[jnp.minimum(target + NY, last)] == mine))
-        linked.append(near)
+        from_here = theirs == mine
+        from_left = has_left & (cluster[jnp.maximum(target - NY, 0)] == mine)
+        from_right = has_right & (cluster[jnp.minimum(target + NY, last)] == mine)
+        linked.append(from_here | from_left | from_right)
+        got_left.append(from_left)
+        got_right.append(from_right)
 
     def pick(step, here, from_left, from_right):
         return lax.select(
@@ -161,7 +164,22 @@
         arriving(k).wait()
         own[k] = fresh[k].astype(jnp.bfloat16)
 
-    for k in range(3):
+    def first_along_y():
+        return [
+            send(own.at[0], raw.at[NY - s - 1], y_send.at[s - 1, 0], y_recv.at[NY - s - 1, 0], at_y(s))
+            for s in range(1, NY)
+        ]
+
+    def first_along_z():
+        return [
+            send(raw, raw_beside.at[0], raw_send.at[0], raw_recv.at[0], right_plane),
+            send(raw, raw_beside.at[1], raw_send.at[1], raw_recv.at[1], left_plane),
+        ]
+
+    cast_passage(0)
+    for copy in first_along_y():
+        copy.start()
+    for k in range(1, 4):
         cast_passage(k)
         share(k)
 
@@ -174,7 +192,7 @@
         own[count + k] = fresh[count + k].astype(jnp.bfloat16)
         return carry
 
-    lax.fori_loop(3, count, cast_rest, 0)
+    lax.fori_loop(4, count, cast_rest, 0)
     lax.fori_loop(0, count, cast_queries, 0)
 
     for part in range(rows // 128):
@@ -183,12 +201,14 @@
         pos_cols[here, :] = jnp.broadcast_to(as_row, (128, 128)).T
         weight_cols[here, :] = jnp.broadcast_to(weight[part : part + 1, :], (128, 128)).T
 
-    relay(0)
-    share(3)
     relay(1)
     share(4)
-    landed(0)
-    add_scores(0, first=True)
+    for copy in first_along_y():
+        copy.wait_recv()
+    relay(2)
+    share(5)
+    landed(1)
+    add_scores(1, first=True)
 
     def passage_step(k, carry):
         relay(k)
@@ -197,7 +217,18 @@
         add_scores(k - 1)
         return carry
 
-    lax.fori_loop(2, count, passage_step, 0)
+    passage_step(3, 0)
+    for copy in first_along_z():
+        copy.start()
+    lax.fori_loop(4, count, passage_step, 0)
+    for copy in first_along_z():
+        copy.wait_recv()
+    for slot in range(1, NY):
+        gathered[slot - 1, 0] = lax.select(
+            got_left[slot], raw_beside[0, slot - 1],
+            lax.select(got_right[slot], raw_beside[1, slot - 1], raw[slot - 1]),
+        )
+    add_scores(0)
     relay(count)
     share(count + 3)
     landed(count - 1)
@@ -276,9 +307,7 @@
         value = nn_dot(coeff[0], own[k])
         for slot in range(1, NY):
             value = value + nn_dot(coeff[slot], gathered[slot - 1, k])
-        query_grad[k] = value
-        start = pl.multiple_of(k * CHUNK, CHUNK)
-        pltpu.make_async_copy(query_grad.at[k], query_grad_hbm.at[:, pl.ds(start, CHUNK)], qg_sem.at[k]).start()
+        query_grad[:, pl.ds(pl.multiple_of(k * CHUNK, CHUNK), CHUNK)] = value
         return carry
 
     lax.fori_loop(0, count, query_grad_step, 0)
@@ -342,18 +371,11 @@
         copy.wait_send()
     loss_ref[...] = value * (1.0 / (rows * planes * NY))
 
-    def passage_grad_out(k):
-        start = pl.multiple_of(k * CHUNK, CHUNK)
-        return pltpu.make_async_copy(
-            passage_grad.at[k], passage_grad_hbm.at[:, pl.ds(start, CHUNK)], pg_sem.at[k]
-        )
-
     def passage_grad_step(k, carry):
         value = nn_dot(coeff_t[0], own[count + k])
         for slot in range(1, NY):
             value = value + nn_dot(coeff_t[slot], gathered[slot - 1, count + k])
-        passage_grad[k] = value
-        passage_grad_out(k).start()
+        passage_grad[:, pl.ds(pl.multiple_of(k * CHUNK, CHUNK), CHUNK)] = value
         return carry
 
     landed(count + 5)
@@ -371,17 +393,9 @@
             copy.wait_send()
         return carry
 
-    lax.fori_loop(0, 2 * count, finish_sends, 0)
-    for copy in coeff_z + coeff_y + [swap, forward]:
+    lax.fori_loop(1, 2 * count, finish_sends, 0)
+    for copy in first_along_y() + first_along_z() + coeff_z + coeff_y + [swap, forward]:
         copy.wait_send()
-
-    def finish_out(k, carry):
-        start = pl.multiple_of(k * CHUNK, CHUNK)
-        pltpu.make_async_copy(query_grad.at[k], query_grad_hbm.at[:, pl.ds(start, CHUNK)], qg_sem.at[k]).wait()
-        passage_grad_out(k).wait()
-        return carry
-
-    lax.fori_loop(0, count, finish_out, 0)
 
 
 def shards(queries, passages, cluster_of_block, positive_row, query_weight):
@@ -397,6 +411,8 @@
         vmem((2, 2 * count, rows, CHUNK), low),
         vmem((NY - 1, 2 * count, rows, CHUNK), low),
         vmem((NY - 1, 2 * count, rows, CHUNK), low),
+        vmem((NY - 1, rows, CHUNK), low),
+        vmem((2, NY - 1, rows, CHUNK), low),
         vmem((rows, NY * rows), full),
         vmem((rows, NY * rows), full),
         vmem((NY, rows, rows), low),
@@ -408,8 +424,6 @@
         vmem((NY, rows, rows), low),
         vmem((rows, 128), full),
         vmem((rows, 128), full),
-        vmem((count, rows, CHUNK), full),
-        vmem((count, rows, CHUNK), full),
         vmem(tile, full),
         vmem((NY,) + tile, full),
         vmem((NZ,) + tile, full),
@@ -426,7 +440,7 @@
         dma((NY,)), dma((NY,)),
         dma((NZ,)), dma((NZ,)),
         dma((NX,)), dma((NX,)),
-        dma((count,)), dma((count,)),
+        dma((2,)), dma((2,)),
     ]
     anywhere = pl.BlockSpec(memory_space=pl.ANY)
     in_vmem = pl.BlockSpec(memory_space=pltpu.VMEM)
@@ -434,14 +448,14 @@
         kernel,
         out_shape=[
             jax.ShapeDtypeStruct(tile, full),
-            jax.ShapeDtypeStruct((rows, width), full),
-            jax.ShapeDtypeStruct((rows, width), full),
+            vmem((rows, width), full),
+            vmem((rows, width), full),
         ],
         in_specs=[anywhere, anywhere, pl.BlockSpec(memory_space=pltpu.SMEM), in_vmem, in_vmem],
-        out_specs=[in_vmem, anywhere, anywhere],
+        out_specs=[in_vmem, in_vmem, in_vmem],
         scratch_shapes=scratch,
         compiler_params=pltpu.CompilerParams(
-            collective_id=0, has_side_effects=True, vmem_limit_bytes=56 * 2**20
+            collective_id=0, has_side_effects=True, vmem_limit_bytes=48 * 2**20
         ),
         cost_estimate=pl.CostEstimate(
             flops=6 * NY * rows * rows * width, bytes_accessed=16 * rows * width, transcendentals=NY * rows * rows

time: 122 us -> 115 us (0.943)
  Pallas kernels: 115 us -> 109 us
    pallas_call x1, Pallas kernels: 115 us -> 109 us  [shards(): pl.pallas_call(kernel, out_shape=[jax.ShapeDtypeStruct(tile, full), vmem(...]
    unnamed x4 -> x8, local copies, waits for them, and re-layouts: 4.61 us -> 4.64 us
where the time goes in v2:
time: 115 us
  Pallas kernels  109 us (95%)
  local copies, waits for them, and re-layouts  5.16 us (4%)
    pallas_call x1, Pallas kernels, shards(): pl.pallas_call(kernel, out_shape=[jax.ShapeDtypeStruct(tile, full), vmem(...  109 us
    unnamed x8, local copies, waits for them, and re-layouts  4.64 us

profile of v2, /device:TPU:1, one launch (start us, length us, event | category | flops | bytes accessed | tf_op | source)
XLA Modules:
  0.0 114.7 jit_solution(16486749511465696654)
XLA Ops:
  0.6 0.0 copy-start
  0.6 0.7 copy-done
  1.3 0.0 copy-start.1
  1.3 0.7 copy-done.1
  2.0 0.0 copy-start.2
  2.0 0.7 copy-done.2
  2.6 108.9 %shard_map.76 = (f32[8,128]{1,0:T(8,128)S(1)}, f32[256,2048]{1,0:T(8,128)S(1)}, f32[256,2048]{1,0:T(8,128)S(1)}) custom-call(f32[256,2048]{1,0:T(8,128)} %query_hbm.1, f32[256,2048]{1,0:T(8,128)} %passage_hbm.1, s32[128]{0:T(128)S(1)} %copy-done.2, s32[2,128]{1,0:T(2,128)S(1)} %bitcast.3, f32[2,128]{1,0:T(2,128)S(1)} %bitcast.4), custom_call_target="tpu_custom_call" | custom-call | flops 3221225472 | bytes 8388608 | tf_op jit(solution)/shard_map/pallas_call | solution.py:447
  111.5 0.5 slice.3
  112.0 1.3 %copy.10 = f32[256,2048]{1,0:T(8,128)} copy(f32[256,2048]{1,0:T(8,128)S(1)} %get-tuple-element.10) | data formatting | bytes 4194304
  113.4 1.3 %copy.11 = f32[256,2048]{1,0:T(8,128)} copy(f32[256,2048]{1,0:T(8,128)S(1)} %get-tuple-element.11) | data formatting | bytes 4194304
Async XLA Ops:
  0.6 0.7 copy-start
  1.3 0.7 copy-start.1
  2.0 0.7 copy-start.2

commit v3 on v2

--- a/solution.py
+++ b/solution.py
@@ -23,14 +23,14 @@
 
 
 def kernel(
-    query_hbm, passage_hbm, cluster, positive, weight,
+    query_hbm, passage_hbm, cluster_hbm, positive_hbm, weight_hbm,
     loss_ref, query_grad, passage_grad,
-    fresh, own, beside, staged, gathered, raw, raw_beside,
+    cluster, positive, weight, fresh, own, beside, staged, gathered, raw, raw_beside,
     score_own, score_other, coeff, coeff_out, coeff_beside, coeff_staged, coeff_got, coeff_fwd, coeff_t,
     pos_cols, weight_cols, loss_tile, loss_y, loss_z, loss_x,
     in_sem, z_send, z_recv, y_send, y_recv, s_send, s_recv,
     cz_send, cz_recv, cy_send, cy_recv, cf_send, cf_recv,
-    ly_send, ly_recv, lz_send, lz_recv, lx_send, lx_recv, raw_send, raw_recv,
+    ly_send, ly_recv, lz_send, lz_recv, lx_send, lx_recv, raw_send, raw_recv, small_sem,
 ):
     rows, width = query_hbm.shape
     count = width // CHUNK
@@ -73,7 +73,16 @@
         arriving_query(k).start()
         return carry
 
-    lax.fori_loop(0, count, start_in, 0)
+    small = [
+        pltpu.make_async_copy(source, target, small_sem.at[i])
+        for i, (source, target) in enumerate(
+            [(cluster_hbm, cluster), (positive_hbm, positive), (weight_hbm, weight)]
+        )
+    ]
+    arriving(0).start()
+    for copy in small:
+        copy.start()
+    lax.fori_loop(1, count, start_in, 0)
     lax.fori_loop(0, count, start_in_query, 0)
 
     barrier = pltpu.get_barrier_semaphore()
@@ -83,6 +92,9 @@
         pl.semaphore_signal(barrier, inc=1, device_id=(peer, core), device_id_type=MESH)
     pl.semaphore_signal(barrier, inc=1, device_id=(me, 1 - core), device_id_type=MESH)
     pl.semaphore_wait(barrier, len(peers) + 1)
+
+    for copy in small:
+        copy.wait()
 
     last = planes * NY - 1
     mine = cluster[me]
@@ -406,6 +418,9 @@
     low, full = jnp.bfloat16, jnp.float32
     tile = (8, 128)
     scratch = [
+        pltpu.SMEM(cluster_of_block.shape, jnp.int32),
+        vmem((rows // 128, 128), jnp.int32),
+        vmem((rows // 128, 128), full),
         vmem((2 * count, rows, CHUNK), full),
         vmem((2 * count, rows, CHUNK), low),
         vmem((2, 2 * count, rows, CHUNK), low),
@@ -441,8 +456,8 @@
         dma((NZ,)), dma((NZ,)),
         dma((NX,)), dma((NX,)),
         dma((2,)), dma((2,)),
+        dma((3,)),
     ]
-    anywhere = pl.BlockSpec(memory_space=pl.ANY)
     in_vmem = pl.BlockSpec(memory_space=pltpu.VMEM)
     loss, query_grad, passage_grad = pl.pallas_call(
         kernel,
@@ -451,7 +466,7 @@
             vmem((rows, width), full),
             vmem((rows, width), full),
         ],
-        in_specs=[anywhere, anywhere, pl.BlockSpec(memory_space=pltpu.SMEM), in_vmem, in_vmem],
+        in_specs=[pl.BlockSpec(memory_space=pltpu.HBM)] * 5,
         out_specs=[in_vmem, in_vmem, in_vmem],
         scratch_shapes=scratch,
         compiler_params=pltpu.CompilerParams(
@@ -461,8 +476,13 @@
             flops=6 * NY * rows * rows * width, bytes_accessed=16 * rows * width, transcendentals=NY * rows * rows
         ),
     )(
-        queries, passages, cluster_of_block,
-        positive_row.reshape(rows // 128, 128), query_weight.reshape(rows // 128, 128),
+        *[
+            pltpu.with_memory_space_constraint(array, pltpu.HBM)
+            for array in (
+                queries, passages, cluster_of_block,
+                positive_row.reshape(rows // 128, 128), query_weight.reshape(rows // 128, 128),
+            )
+        ]
     )
     return loss[0, 0], query_grad, passage_grad
 

time: 115 us -> 112 us (0.974)
  local copies, waits for them, and re-layouts: 5.16 us -> 3.15 us
    unnamed x8 -> x2, local copies, waits for them, and re-layouts: 4.64 us -> 2.64 us
where the time goes in v3:
time: 112 us
  Pallas kernels  109 us (97%)
  local copies, waits for them, and re-layouts  3.15 us (3%)
    pallas_call x1, Pallas kernels, shards(): pl.pallas_call(kernel, out_shape=[jax.ShapeDtypeStruct(tile, full), vmem(...  109 us
    unnamed x2, local copies, waits for them, and re-layouts  2.64 us

profile of v3, /device:TPU:1, one launch (start us, length us, event | category | flops | bytes accessed | tf_op | source)
XLA Modules:
  0.0 112.3 jit_solution(9722729802887242309)
XLA Ops:
  0.6 108.5 %shard_map.76 = (f32[8,128]{1,0:T(8,128)S(1)}, f32[256,2048]{1,0:T(8,128)S(1)}, f32[256,2048]{1,0:T(8,128)S(1)}) custom-call(f32[256,2048]{1,0:T(8,128)} %query_hbm.1, f32[256,2048]{1,0:T(8,128)} %passage_hbm.1, s32[128]{0:T(128)} %cluster_hbm.1, s32[2,128]{1,0:T(2,128)} %bitcast.3, f32[2,128]{1,0:T(2,128)} %bitcast.4), custom_call_target="tpu_custom_call" | custom-call | flops 3221225472 | bytes 8388608 | tf_op jit(solution)/shard_map/pallas_call | solution.py:462
  109.2 0.5 slice.3
  109.7 1.3 %copy.10 = f32[256,2048]{1,0:T(8,128)} copy(f32[256,2048]{1,0:T(8,128)S(1)} %get-tuple-element.10) | data formatting | bytes 4194304
  111.0 1.3 %copy.11 = f32[256,2048]{1,0:T(8,128)} copy(f32[256,2048]{1,0:T(8,128)S(1)} %get-tuple-element.11) | data formatting | bytes 4194304

commit v4 on v3

--- a/solution.py
+++ b/solution.py
@@ -26,11 +26,12 @@
     query_hbm, passage_hbm, cluster_hbm, positive_hbm, weight_hbm,
     loss_ref, query_grad, passage_grad,
     cluster, positive, weight, fresh, own, beside, staged, gathered, raw, raw_beside,
-    score_own, score_other, coeff, coeff_out, coeff_beside, coeff_staged, coeff_got, coeff_fwd, coeff_t,
+    passed, across, ring_out, ring_in,
+    score_own, score_other, coeff, coeff_out, coeff_beside, coeff_staged, coeff_got, coeff_fwd, coeff_t, middle_t,
     pos_cols, weight_cols, loss_tile, loss_y, loss_z, loss_x,
     in_sem, z_send, z_recv, y_send, y_recv, s_send, s_recv,
     cz_send, cz_recv, cy_send, cy_recv, cf_send, cf_recv,
-    ly_send, ly_recv, lz_send, lz_recv, lx_send, lx_recv, raw_send, raw_recv, small_sem,
+    ly_send, ly_recv, lz_send, lz_recv, lx_send, lx_recv, raw_send, raw_recv, small_sem, ring_send, ring_recv, hop_send, hop_recv,
 ):
     rows, width = query_hbm.shape
     count = width // CHUNK
@@ -116,6 +117,18 @@
         got_left.append(from_left)
         got_right.append(from_right)
 
+    def same(step):
+        there = me + step
+        inside = (there >= 0) & (there <= last)
+        return inside & (cluster[jnp.clip(there, 0, last)] == mine)
+
+    near_up, near_down = same(1), same(-1)
+    far_up, far_down = same(2), same(-2)
+    middle = near_up & near_down & jnp.logical_not(far_up) & jnp.logical_not(far_down)
+    top_end = near_down & far_down & jnp.logical_not(same(-3)) & jnp.logical_not(near_up)
+    low_end = near_up & far_up & jnp.logical_not(same(3)) & jnp.logical_not(near_down)
+    from_beside = [want_left[0] | want_right[0], want_left[2] | want_right[2]]
+
     def pick(step, here, from_left, from_right):
         return lax.select(
             want_left[step - 1], from_left, lax.select(want_right[step - 1], from_right, here)
@@ -222,17 +235,88 @@
     landed(1)
     add_scores(1, first=True)
 
-    def passage_step(k, carry):
+    part = count // 2
+    hop_place = [
+        jnp.where(y == NY - 1, right_plane, left_plane),
+        jnp.where(y == 0, left_plane, right_plane),
+    ]
+    wraps = [y == NY - 1, y == 0]
+    steps = [1, NY - 1]
+
+    def ring(way, q):
+        return send(
+            ring_out.at[way, q], ring_in.at[way, q], ring_send.at[way, q], ring_recv.at[way, q], at_y(steps[way])
+        )
+
+    def hop(way, j):
+        return send(
+            passed.at[way, j], across.at[way, j], hop_send.at[way, j], hop_recv.at[way, j], hop_place[way]
+        )
+
+    def query_chunk(way, q):
+        return count + (q + part) % count if way == 0 else count + q
+
+    def ring_first(q):
+        for k in (q, q + part):
+            for copy in along_z(count + k):
+                copy.wait_recv()
+        for way in range(2):
+            k = query_chunk(way, q)
+            ring_out[way, q] = pick(steps[way], own[k], beside[0, k], beside[1, k])
+            ring(way, q).start()
+
+    def ring_landed(q):
+        for way in range(2):
+            ring(way, q).wait_recv()
+
+    def pass_second(j):
+        for way in range(2):
+            passed[way, j] = lax.select(middle, ring_in[way, j], own[query_chunk(way, part + j)])
+
+            @pl.when(wraps[way])
+            def _():
+                hop(way, j).start()
+
+    def ring_second(j):
+        q = part + j
+        for way in range(2):
+            k = query_chunk(way, q)
+            ring_out[way, q] = pick(steps[way], passed[way, j], beside[0, k], beside[1, k])
+
+            @pl.when(wraps[way])
+            def _():
+                hop(way, j).wait_recv()
+                ring_out[way, q] = lax.select(from_beside[way], across[way, j], passed[way, j])
+
+            ring(way, q).start()
+
+    def pass_last(j):
+        for way in range(2):
+            k = query_chunk(way, part + j)
+            terms = nn_dot(middle_t[way], own[k]) + nn_dot(middle_t[2 + way], ring_in[way, part + j])
+            passed[way, part + j] = lax.select(middle, terms.astype(jnp.bfloat16), ring_in[way, j])
+            hop(way, part + j).start()
+
+    def ring_last(j):
+        q = count + j
+        for way in range(2):
+            hop(way, part + j).wait_recv()
+            ring_out[way, q] = lax.select(from_beside[way], across[way, part + j], passed[way, part + j])
+            ring(way, q).start()
+
+    def passage_step(k, shares):
         relay(k)
-        share(k + 3)
+        for share_now in shares:
+            share(share_now)
         landed(k - 1)
         add_scores(k - 1)
-        return carry
-
-    passage_step(3, 0)
+
+    passage_step(3, [6])
     for copy in first_along_z():
         copy.start()
-    lax.fori_loop(4, count, passage_step, 0)
+    passage_step(4, [7])
+    for k in range(5, count):
+        passage_step(k, [count + k - 5, count + part + k - 5])
     for copy in first_along_z():
         copy.wait_recv()
     for slot in range(1, NY):
@@ -241,14 +325,15 @@
             lax.select(got_right[slot], raw_beside[1, slot - 1], raw[slot - 1]),
         )
     add_scores(0)
-    relay(count)
-    share(count + 3)
+    share(count + part - 1)
+    share(2 * count - 1)
+    ring_first(0)
     landed(count - 1)
+    ring_first(1)
     add_scores(count - 1)
     swap = send(score_own, score_other, s_send, s_recv, me, 1 - core)
     swap.start()
-    relay(count + 1)
-    share(count + 4)
+    ring_first(2)
     swap.wait_recv()
 
     scale = 3.0 / math.sqrt(2 * width)
@@ -311,9 +396,10 @@
     for copy in loss_along_y:
         copy.start()
 
-    landed(count)
-    relay(count + 2)
-    share(count + 5)
+    ring_first(3)
+    for j in range(2):
+        ring_landed(j)
+        pass_second(j)
 
     def query_grad_step(k, carry):
         value = nn_dot(coeff[0], own[k])
@@ -326,20 +412,22 @@
 
     for copy in coeff_z:
         copy.wait_recv()
-    for s in range(1, NY):
-        coeff_staged[s - 1] = pick(s, coeff_out[s - 1], coeff_beside[0, s - 1], coeff_beside[1, s - 1])
+    for place, (s, tile) in enumerate([(1, 1), (1, 2), (2, 2), (3, 3), (3, 2)]):
+        coeff_staged[place] = pick(s, coeff_out[tile - 1], coeff_beside[0, tile - 1], coeff_beside[1, tile - 1])
     coeff_y = [
-        send(
-            coeff_staged.at[s - 1], coeff_got.at[NY - s - 1], cy_send.at[s - 1], cy_recv.at[NY - s - 1], at_y(s)
-        )
-        for s in range(1, NY)
+        send(coeff_staged.at[0:2], coeff_got.at[3:5], cy_send.at[0], cy_recv.at[2], at_y(1)),
+        send(coeff_staged.at[2], coeff_got.at[2], cy_send.at[1], cy_recv.at[1], at_y(2)),
+        send(coeff_staged.at[3:5], coeff_got.at[0:2], cy_send.at[2], cy_recv.at[0], at_y(3)),
     ]
     for copy in coeff_y:
         copy.start()
 
-    landed(count + 1)
-    relay(count + 3)
-    share(count + 6)
+    ring_second(0)
+    ring_landed(2)
+    pass_second(2)
+    ring_second(1)
+    ring_landed(3)
+    pass_second(3)
     value = collect(loss_y, ly_recv, y, NY)
     for copy in loss_along_y:
         copy.wait_send()
@@ -347,14 +435,43 @@
     loss_along_z = spread(loss_z, lz_send, lz_recv, z, NZ, at_z)
     for copy in loss_along_z:
         copy.start()
-
-    landed(count + 2)
-    relay(count + 4)
-    share(count + 7)
+    ring_second(2)
     for copy in coeff_y:
         copy.wait_recv()
     forward = send(coeff_got, coeff_fwd, cf_send, cf_recv, me, 1 - core)
     forward.start()
+    ring_second(3)
+
+    def turned(tile):
+        return tile.astype(jnp.float32).T
+
+    coeff_t[0] = turned(coeff[0]).astype(jnp.bfloat16)
+    middle_t[0] = turned(coeff[1]).astype(jnp.bfloat16)
+    middle_t[1] = turned(coeff[3]).astype(jnp.bfloat16)
+    forward.wait_recv()
+    first_half = core == 0
+
+    def whole(place):
+        got, fwd = coeff_got[place], coeff_fwd[place]
+        return turned(
+            jnp.concatenate([lax.select(first_half, got, fwd), lax.select(first_half, fwd, got)], axis=0)
+        )
+
+    middle_t[2] = whole(4).astype(jnp.bfloat16)
+    middle_t[3] = whole(1).astype(jnp.bfloat16)
+    ring_landed(4)
+    pass_last(0)
+    ring_landed(5)
+    pass_last(1)
+    for slot, place in ((1, 0), (2, 2), (3, 3)):
+        tile = whole(place)
+        coeff_t[slot] = lax.select(linked[slot], tile, jnp.zeros_like(tile)).astype(jnp.bfloat16)
+    ring_last(0)
+    ring_landed(6)
+    pass_last(2)
+    ring_last(1)
+    ring_landed(7)
+    pass_last(3)
     value = collect(loss_z, lz_recv, z, NZ)
     for copy in loss_along_z:
         copy.wait_send()
@@ -362,50 +479,68 @@
     loss_along_x = spread(loss_x, lx_send, lx_recv, x, NX, at_x)
     for copy in loss_along_x:
         copy.start()
-
-    landed(count + 3)
-    relay(count + 5)
-    forward.wait_recv()
-
-    coeff_t[0] = coeff[0].astype(jnp.float32).T.astype(jnp.bfloat16)
-    first_half = core == 0
-    for slot in range(1, NY):
-        got, fwd = coeff_got[slot - 1], coeff_fwd[slot - 1]
-        tile = jnp.concatenate([lax.select(first_half, got, fwd), lax.select(first_half, fwd, got)], axis=0)
-        tile = tile.astype(jnp.float32).T
-        tile = lax.select(linked[slot], tile, jnp.zeros_like(tile))
-        coeff_t[slot] = tile.astype(jnp.bfloat16)
-
-    landed(count + 4)
-    relay(count + 6)
-    value = collect(loss_x, lx_recv, x, NX)
-    for copy in loss_along_x:
-        copy.wait_send()
-    loss_ref[...] = value * (1.0 / (rows * planes * NY))
-
-    def passage_grad_step(k, carry):
-        value = nn_dot(coeff_t[0], own[count + k])
-        for slot in range(1, NY):
-            value = value + nn_dot(coeff_t[slot], gathered[slot - 1, count + k])
-        passage_grad[:, pl.ds(pl.multiple_of(k * CHUNK, CHUNK), CHUNK)] = value
-        return carry
-
-    landed(count + 5)
-    relay(count + 7)
-    lax.fori_loop(0, 6, passage_grad_step, 0)
-    landed(count + 6)
-    passage_grad_step(6, 0)
-    landed(count + 7)
-    passage_grad_step(7, 0)
-
-    def finish_sends(k, carry):
+    ring_last(2)
+    ring_last(3)
+
+    def passage_grad_chunk(k, start):
+        j = k % part
+        up, down = ring_in[0, (k + part) % count], ring_in[1, k]
+        far = ring_in[1 if start else 0, count + j]
+        relayed = ring_in[1 if start else 0, part + j]
+        near_end, far_end = (low_end, top_end) if start else (top_end, low_end)
+        done = ring_in[0 if start else 1, count + j].astype(jnp.float32)
+        from_up = nn_dot(coeff_t[NY - 1], up)
+        from_down = nn_dot(coeff_t[1], down)
+        if start:
+            from_up = lax.select(far_end, done, from_up)
+        else:
+            from_down = lax.select(far_end, done, from_down)
+        opposite = nn_dot(coeff_t[2], lax.select(near_end, relayed, far))
+        opposite = lax.select(far_end, jnp.zeros_like(opposite), opposite)
+        value = nn_dot(coeff_t[0], own[count + k]) + from_up + from_down + opposite
+        passage_grad[:, k * CHUNK : (k + 1) * CHUNK] = value
+
+    for j in range(part):
+        ring_landed(count + j)
+        passage_grad_chunk(j, True)
+        passage_grad_chunk(part + j, False)
+        if j == 0:
+            value = collect(loss_x, lx_recv, x, NX)
+            for copy in loss_along_x:
+                copy.wait_send()
+            loss_ref[...] = value * (1.0 / (rows * planes * NY))
+
+    def finish_shares(k, carry):
         for copy in along_z(k):
             copy.wait_send()
+        return carry
+
+    def finish_chunks(k, carry):
         for copy in along_y(k):
             copy.wait_send()
         return carry
 
-    lax.fori_loop(1, 2 * count, finish_sends, 0)
+    def finish_ring(q, carry):
+        for way in range(2):
+            ring(way, q).wait_send()
+        return carry
+
+    def finish_hops(j, carry):
+        for way in range(2):
+            hop(way, j).wait_send()
+        return carry
+
+    lax.fori_loop(1, 2 * count, finish_shares, 0)
+    lax.fori_loop(1, count, finish_chunks, 0)
+    lax.fori_loop(0, count + part, finish_ring, 0)
+    for way in range(2):
+
+        @pl.when(wraps[way])
+        def _():
+            for j in range(part):
+                hop(way, j).wait_send()
+
+    lax.fori_loop(part, count, finish_hops, 0)
     for copy in first_along_y() + first_along_z() + coeff_z + coeff_y + [swap, forward]:
         copy.wait_send()
 
@@ -417,6 +552,7 @@
     vmem = pltpu.VMEM
     low, full = jnp.bfloat16, jnp.float32
     tile = (8, 128)
+    slots = count + count // 2
     scratch = [
         pltpu.SMEM(cluster_of_block.shape, jnp.int32),
         vmem((rows // 128, 128), jnp.int32),
@@ -424,18 +560,23 @@
         vmem((2 * count, rows, CHUNK), full),
         vmem((2 * count, rows, CHUNK), low),
         vmem((2, 2 * count, rows, CHUNK), low),
-        vmem((NY - 1, 2 * count, rows, CHUNK), low),
-        vmem((NY - 1, 2 * count, rows, CHUNK), low),
+        vmem((NY - 1, count, rows, CHUNK), low),
+        vmem((NY - 1, count, rows, CHUNK), low),
         vmem((NY - 1, rows, CHUNK), low),
         vmem((2, NY - 1, rows, CHUNK), low),
+        vmem((2, count, rows, CHUNK), low),
+        vmem((2, count, rows, CHUNK), low),
+        vmem((2, slots, rows, CHUNK), low),
+        vmem((2, slots, rows, CHUNK), low),
         vmem((rows, NY * rows), full),
         vmem((rows, NY * rows), full),
         vmem((NY, rows, rows), low),
         vmem((NY - 1, rows // 2, rows), low),
         vmem((2, NY - 1, rows // 2, rows), low),
-        vmem((NY - 1, rows // 2, rows), low),
-        vmem((NY - 1, rows // 2, rows), low),
-        vmem((NY - 1, rows // 2, rows), low),
+        vmem((NY + 1, rows // 2, rows), low),
+        vmem((NY + 1, rows // 2, rows), low),
+        vmem((NY + 1, rows // 2, rows), low),
+        vmem((NY, rows, rows), low),
         vmem((NY, rows, rows), low),
         vmem((rows, 128), full),
         vmem((rows, 128), full),
@@ -446,8 +587,8 @@
         dma((2 * count,)),
         dma((2, 2 * count)),
         dma((2, 2 * count)),
-        dma((NY - 1, 2 * count)),
-        dma((NY - 1, 2 * count)),
+        dma((NY - 1, count)),
+        dma((NY - 1, count)),
         dma, dma,
         dma((2,)), dma((2,)),
         dma((NY - 1,)), dma((NY - 1,)),
@@ -457,6 +598,8 @@
         dma((NX,)), dma((NX,)),
         dma((2,)), dma((2,)),
         dma((3,)),
+        dma((2, slots)), dma((2, slots)),
+        dma((2, count)), dma((2, count)),
     ]
     in_vmem = pl.BlockSpec(memory_space=pltpu.VMEM)
     loss, query_grad, passage_grad = pl.pallas_call(

time: 112 us -> 117 us (1.045); the launches traced: 112 us -> 115 us
  Pallas kernels: 109 us -> 111 us
    pallas_call x1, Pallas kernels: 109 us -> 111 us  [shards(): pl.pallas_call(kernel, out_shape=[jax.ShapeDtypeStruct(tile, full), vmem(...]
where the time goes in v4:
time: 117 us; the launch traced here: 115 us
  Pallas kernels  111 us (95%)
  local copies, waits for them, and re-layouts  3.15 us (3%)
    pallas_call x1, Pallas kernels, shards(): pl.pallas_call(kernel, out_shape=[jax.ShapeDtypeStruct(tile, full), vmem(...  111 us
    unnamed x2, local copies, waits for them, and re-layouts  2.64 us

profile of v4, /device:TPU:1, one launch (start us, length us, event | category | flops | bytes accessed | tf_op | source)
XLA Modules:
  0.0 114.6 jit_solution(6762670370197701553)
XLA Ops:
  0.6 110.8 %shard_map.76 = (f32[8,128]{1,0:T(8,128)S(1)}, f32[256,2048]{1,0:T(8,128)S(1)}, f32[256,2048]{1,0:T(8,128)S(1)}) custom-call(f32[256,2048]{1,0:T(8,128)} %query_hbm.1, f32[256,2048]{1,0:T(8,128)} %passage_hbm.1, s32[128]{0:T(128)} %cluster_hbm.1, s32[2,128]{1,0:T(2,128)} %bitcast.3, f32[2,128]{1,0:T(2,128)} %bitcast.4), custom_call_target="tpu_custom_call" | custom-call | flops 3221225472 | bytes 8388608 | tf_op jit(solution)/shard_map/pallas_call | solution.py:605
  111.4 0.5 slice.3
  112.0 1.3 %copy.10 = f32[256,2048]{1,0:T(8,128)} copy(f32[256,2048]{1,0:T(8,128)S(1)} %get-tuple-element.10) | data formatting | bytes 4194304
  113.3 1.3 %copy.11 = f32[256,2048]{1,0:T(8,128)} copy(f32[256,2048]{1,0:T(8,128)S(1)} %get-tuple-element.11) | data formatting | bytes 4194304

commit v5 on v4

--- a/solution.py
+++ b/solution.py
@@ -55,6 +55,8 @@
 
     left_plane = ((plane + planes - 1) % planes) * NY + y
     right_plane = ((plane + 1) % planes) * NY + y
+    one_way = [jnp.where(y + s < NY, right_plane, left_plane) for s in range(1, NY)]
+    other_way = [jnp.where(y + s < NY, left_plane, right_plane) for s in range(1, NY)]
 
     def arriving(k):
         start = pl.multiple_of(k * CHUNK, CHUNK)
@@ -104,7 +106,7 @@
     has_left = plane > 0
     has_right = plane < planes - 1
     want_left, want_right, linked = [], [], [None]
-    got_left, got_right = [None], [None]
+    got_beside = [None]
     for step in range(1, NY):
         target = at_y(step)
         theirs = cluster[target]
@@ -114,8 +116,7 @@
         from_left = has_left & (cluster[jnp.maximum(target - NY, 0)] == mine)
         from_right = has_right & (cluster[jnp.minimum(target + NY, last)] == mine)
         linked.append(from_here | from_left | from_right)
-        got_left.append(from_left)
-        got_right.append(from_right)
+        got_beside.append(from_left | from_right)
 
     def same(step):
         there = me + step
@@ -197,8 +198,8 @@
 
     def first_along_z():
         return [
-            send(raw, raw_beside.at[0], raw_send.at[0], raw_recv.at[0], right_plane),
-            send(raw, raw_beside.at[1], raw_send.at[1], raw_recv.at[1], left_plane),
+            send(raw.at[s - 1], raw_beside.at[s - 1], raw_send.at[s - 1], raw_recv.at[s - 1], one_way[s - 1])
+            for s in range(1, NY)
         ]
 
     cast_passage(0)
@@ -248,9 +249,17 @@
             ring_out.at[way, q], ring_in.at[way, q], ring_send.at[way, q], ring_recv.at[way, q], at_y(steps[way])
         )
 
-    def hop(way, j):
+    def hop(way, j, relayed=False):
+        source = ring_in.at[way, j - part] if relayed else passed.at[way, j]
+        return send(source, across.at[way, j], hop_send.at[way, j], hop_recv.at[way, j], hop_place[way])
+
+    late_place = [right_plane, left_plane]
+    late_columns = [y == 0, y == NY - 1]
+    late_wanted = [near_down, near_up]
+
+    def late(way, j):
         return send(
-            passed.at[way, j], across.at[way, j], hop_send.at[way, j], hop_recv.at[way, j], hop_place[way]
+            ring_in.at[way, part + j], across.at[way, j], hop_send.at[way, j], hop_recv.at[way, j], late_place[way]
         )
 
     def query_chunk(way, q):
@@ -269,33 +278,56 @@
         for way in range(2):
             ring(way, q).wait_recv()
 
-    def pass_second(j):
-        for way in range(2):
-            passed[way, j] = lax.select(middle, ring_in[way, j], own[query_chunk(way, part + j)])
+    def pass_relayed(j):
+        for way in range(2):
+
+            @pl.when(jnp.logical_not(wraps[way]))
+            def _():
+                hop(way, part + j, True).start()
+
+    def ring_second(j):
+        q = part + j
+        for way in range(2):
+            k = query_chunk(way, q)
+            here = lax.select(middle, ring_in[way, j], own[k])
+            s = steps[way] - 1
+            inside = jnp.logical_not(wraps[way])
+            here = lax.select(inside & want_right[s], beside[1, k], here)
+            ring_out[way, q] = lax.select(inside & want_left[s], beside[0, k], here)
+            ring(way, q).start()
+
+    def last_content(way, j):
+        k = query_chunk(way, part + j)
+        terms = nn_dot(middle_t[way], own[k]) + nn_dot(middle_t[2 + way], ring_in[way, part + j])
+        passed[way, part + j] = lax.select(middle, terms.astype(jnp.bfloat16), ring_in[way, j])
+
+    def begin_last(j):
+        for way in range(2):
+
+            @pl.when(late_columns[way])
+            def _():
+                late(way, j).start()
+
+        for way in range(2):
 
             @pl.when(wraps[way])
             def _():
-                hop(way, j).start()
-
-    def ring_second(j):
-        q = part + j
-        for way in range(2):
-            k = query_chunk(way, q)
-            ring_out[way, q] = pick(steps[way], passed[way, j], beside[0, k], beside[1, k])
-
-            @pl.when(wraps[way])
+                last_content(way, j)
+                hop(way, part + j).start()
+
+    def finish_last(j):
+        for way in range(2):
+
+            @pl.when(late_columns[way])
             def _():
-                hop(way, j).wait_recv()
-                ring_out[way, q] = lax.select(from_beside[way], across[way, j], passed[way, j])
-
-            ring(way, q).start()
-
-    def pass_last(j):
-        for way in range(2):
-            k = query_chunk(way, part + j)
-            terms = nn_dot(middle_t[way], own[k]) + nn_dot(middle_t[2 + way], ring_in[way, part + j])
-            passed[way, part + j] = lax.select(middle, terms.astype(jnp.bfloat16), ring_in[way, j])
-            hop(way, part + j).start()
+                late(way, j).wait()
+                ring_in[way, part + j] = lax.select(late_wanted[way], across[way, j], ring_in[way, part + j])
+
+        for way in range(2):
+
+            @pl.when(jnp.logical_not(wraps[way]))
+            def _():
+                last_content(way, j)
 
     def ring_last(j):
         q = count + j
@@ -320,10 +352,7 @@
     for copy in first_along_z():
         copy.wait_recv()
     for slot in range(1, NY):
-        gathered[slot - 1, 0] = lax.select(
-            got_left[slot], raw_beside[0, slot - 1],
-            lax.select(got_right[slot], raw_beside[1, slot - 1], raw[slot - 1]),
-        )
+        gathered[slot - 1, 0] = lax.select(got_beside[slot], raw_beside[slot - 1], raw[slot - 1])
     add_scores(0)
     share(count + part - 1)
     share(2 * count - 1)
@@ -370,8 +399,8 @@
     for s in range(1, NY):
         coeff_out[s - 1] = coeff[s, my_half, :]
     coeff_z = [
-        send(coeff_out, coeff_beside.at[0], cz_send.at[0], cz_recv.at[0], right_plane),
-        send(coeff_out, coeff_beside.at[1], cz_send.at[1], cz_recv.at[1], left_plane),
+        send(coeff_out.at[s - 1], coeff_beside.at[s - 1], cz_send.at[s - 1], cz_recv.at[s - 1], other_way[s - 1])
+        for s in range(1, NY)
     ]
     for copy in coeff_z:
         copy.start()
@@ -399,7 +428,7 @@
     ring_first(3)
     for j in range(2):
         ring_landed(j)
-        pass_second(j)
+        pass_relayed(j)
 
     def query_grad_step(k, carry):
         value = nn_dot(coeff[0], own[k])
@@ -413,7 +442,9 @@
     for copy in coeff_z:
         copy.wait_recv()
     for place, (s, tile) in enumerate([(1, 1), (1, 2), (2, 2), (3, 3), (3, 2)]):
-        coeff_staged[place] = pick(s, coeff_out[tile - 1], coeff_beside[0, tile - 1], coeff_beside[1, tile - 1])
+        coeff_staged[place] = lax.select(
+            want_left[s - 1] | want_right[s - 1], coeff_beside[tile - 1], coeff_out[tile - 1]
+        )
     coeff_y = [
         send(coeff_staged.at[0:2], coeff_got.at[3:5], cy_send.at[0], cy_recv.at[2], at_y(1)),
         send(coeff_staged.at[2], coeff_got.at[2], cy_send.at[1], cy_recv.at[1], at_y(2)),
@@ -424,10 +455,10 @@
 
     ring_second(0)
     ring_landed(2)
-    pass_second(2)
+    pass_relayed(2)
     ring_second(1)
     ring_landed(3)
-    pass_second(3)
+    pass_relayed(3)
     value = collect(loss_y, ly_recv, y, NY)
     for copy in loss_along_y:
         copy.wait_send()
@@ -460,18 +491,22 @@
     middle_t[2] = whole(4).astype(jnp.bfloat16)
     middle_t[3] = whole(1).astype(jnp.bfloat16)
     ring_landed(4)
-    pass_last(0)
-    ring_landed(5)
-    pass_last(1)
+    begin_last(0)
     for slot, place in ((1, 0), (2, 2), (3, 3)):
         tile = whole(place)
         coeff_t[slot] = lax.select(linked[slot], tile, jnp.zeros_like(tile)).astype(jnp.bfloat16)
+    ring_landed(5)
+    begin_last(1)
+    finish_last(0)
     ring_last(0)
     ring_landed(6)
-    pass_last(2)
+    begin_last(2)
+    finish_last(1)
     ring_last(1)
     ring_landed(7)
-    pass_last(3)
+    begin_last(3)
+    finish_last(2)
+    ring_last(2)
     value = collect(loss_z, lz_recv, z, NZ)
     for copy in loss_along_z:
         copy.wait_send()
@@ -479,7 +514,7 @@
     loss_along_x = spread(loss_x, lx_send, lx_recv, x, NX, at_x)
     for copy in loss_along_x:
         copy.start()
-    ring_last(2)
+    finish_last(3)
     ring_last(3)
 
     def passage_grad_chunk(k, start):
@@ -533,13 +568,6 @@
     lax.fori_loop(1, 2 * count, finish_shares, 0)
     lax.fori_loop(1, count, finish_chunks, 0)
     lax.fori_loop(0, count + part, finish_ring, 0)
-    for way in range(2):
-
-        @pl.when(wraps[way])
-        def _():
-            for j in range(part):
-                hop(way, j).wait_send()
-
     lax.fori_loop(part, count, finish_hops, 0)
     for copy in first_along_y() + first_along_z() + coeff_z + coeff_y + [swap, forward]:
         copy.wait_send()
@@ -563,7 +591,7 @@
         vmem((NY - 1, count, rows, CHUNK), low),
         vmem((NY - 1, count, rows, CHUNK), low),
         vmem((NY - 1, rows, CHUNK), low),
-        vmem((2, NY - 1, rows, CHUNK), low),
+        vmem((NY - 1, rows, CHUNK), low),
         vmem((2, count, rows, CHUNK), low),
         vmem((2, count, rows, CHUNK), low),
         vmem((2, slots, rows, CHUNK), low),
@@ -572,7 +600,7 @@
         vmem((rows, NY * rows), full),
         vmem((NY, rows, rows), low),
         vmem((NY - 1, rows // 2, rows), low),
-        vmem((2, NY - 1, rows // 2, rows), low),
+        vmem((NY - 1, rows // 2, rows), low),
         vmem((NY + 1, rows // 2, rows), low),
         vmem((NY + 1, rows // 2, rows), low),
         vmem((NY + 1, rows // 2, rows), low),
@@ -590,13 +618,13 @@
         dma((NY - 1, count)),
         dma((NY - 1, count)),
         dma, dma,
-        dma((2,)), dma((2,)),
+        dma((NY - 1,)), dma((NY - 1,)),
         dma((NY - 1,)), dma((NY - 1,)),
         dma, dma,
         dma((NY,)), dma((NY,)),
         dma((NZ,)), dma((NZ,)),
         dma((NX,)), dma((NX,)),
-        dma((2,)), dma((2,)),
+        dma((NY - 1,)), dma((NY - 1,)),
         dma((3,)),
         dma((2, slots)), dma((2, slots)),
         dma((2, count)), dma((2, count)),

time: 117 us -> 109 us (0.932); the launches traced: 115 us -> 109 us
  Pallas kernels: 111 us -> 105 us
    pallas_call x1, Pallas kernels: 111 us -> 105 us  [shards(): pl.pallas_call(kernel, out_shape=[jax.ShapeDtypeStruct(tile, full), vmem(...]
where the time goes in v5:
time: 109 us
  Pallas kernels  105 us (96%)
  local copies, waits for them, and re-layouts  3.15 us (3%)
    pallas_call x1, Pallas kernels, shards(): pl.pallas_call(kernel, out_shape=[jax.ShapeDtypeStruct(tile, full), vmem(...  105 us
    unnamed x2, local copies, waits for them, and re-layouts  2.64 us

profile of v5, /device:TPU:1, one launch (start us, length us, event | category | flops | bytes accessed | tf_op | source)
XLA Modules:
  0.0 108.7 jit_solution(2760709568061331750)
XLA Ops:
  0.6 104.9 %shard_map.76 = (f32[8,128]{1,0:T(8,128)S(1)}, f32[256,2048]{1,0:T(8,128)S(1)}, f32[256,2048]{1,0:T(8,128)S(1)}) custom-call(f32[256,2048]{1,0:T(8,128)} %query_hbm.1, f32[256,2048]{1,0:T(8,128)} %passage_hbm.1, s32[128]{0:T(128)} %cluster_hbm.1, s32[2,128]{1,0:T(2,128)} %bitcast.3, f32[2,128]{1,0:T(2,128)} %bitcast.4), custom_call_target="tpu_custom_call" | custom-call | flops 3221225472 | bytes 8388608 | tf_op jit(solution)/shard_map/pallas_call | solution.py:633
  105.6 0.5 slice.3
  106.1 1.3 %copy.10 = f32[256,2048]{1,0:T(8,128)} copy(f32[256,2048]{1,0:T(8,128)S(1)} %get-tuple-element.10) | data formatting | bytes 4194304
  107.4 1.3 %copy.11 = f32[256,2048]{1,0:T(8,128)} copy(f32[256,2048]{1,0:T(8,128)S(1)} %get-tuple-element.11) | data formatting | bytes 4194304

commit v6 on v5

--- a/solution.py
+++ b/solution.py
@@ -12,6 +12,7 @@
 NY, NZ, NX = 4, 8, 4
 CHUNK = 256
 GROUP = 32
+EASY = 1
 
 
 def nt_dot(left, right):
@@ -26,12 +27,13 @@
     query_hbm, passage_hbm, cluster_hbm, positive_hbm, weight_hbm,
     loss_ref, query_grad, passage_grad,
     cluster, positive, weight, fresh, own, beside, staged, gathered, raw, raw_beside,
-    passed, across, ring_out, ring_in,
+    passed, across, ring_out, ring_in, late_in,
     score_own, score_other, coeff, coeff_out, coeff_beside, coeff_staged, coeff_got, coeff_fwd, coeff_t, middle_t,
-    pos_cols, weight_cols, loss_tile, loss_y, loss_z, loss_x,
+    pos_cols, weight_cols, loss_tile, loss_core, loss_y, loss_z, loss_x,
     in_sem, z_send, z_recv, y_send, y_recv, s_send, s_recv,
     cz_send, cz_recv, cy_send, cy_recv, cf_send, cf_recv,
     ly_send, ly_recv, lz_send, lz_recv, lx_send, lx_recv, raw_send, raw_recv, small_sem, ring_send, ring_recv, hop_send, hop_recv,
+    late_send, late_recv, ch_send, ch_recv, lc_send, lc_recv,
 ):
     rows, width = query_hbm.shape
     count = width // CHUNK
@@ -250,7 +252,7 @@
         )
 
     def hop(way, j, relayed=False):
-        source = ring_in.at[way, j - part] if relayed else passed.at[way, j]
+        source = ring_in.at[way, j] if relayed else passed.at[way, j]
         return send(source, across.at[way, j], hop_send.at[way, j], hop_recv.at[way, j], hop_place[way])
 
     late_place = [right_plane, left_plane]
@@ -259,7 +261,7 @@
 
     def late(way, j):
         return send(
-            ring_in.at[way, part + j], across.at[way, j], hop_send.at[way, j], hop_recv.at[way, j], late_place[way]
+            ring_in.at[way, part + j], late_in.at[way, j], late_send.at[way, j], late_recv.at[way, j], late_place[way]
         )
 
     def query_chunk(way, q):
@@ -283,7 +285,7 @@
 
             @pl.when(jnp.logical_not(wraps[way]))
             def _():
-                hop(way, part + j, True).start()
+                hop(way, j, True).start()
 
     def ring_second(j):
         q = part + j
@@ -299,30 +301,34 @@
     def last_content(way, j):
         k = query_chunk(way, part + j)
         terms = nn_dot(middle_t[way], own[k]) + nn_dot(middle_t[2 + way], ring_in[way, part + j])
-        passed[way, part + j] = lax.select(middle, terms.astype(jnp.bfloat16), ring_in[way, j])
-
-    def begin_last(j):
+        passed[way, j] = lax.select(middle, terms.astype(jnp.bfloat16), ring_in[way, j])
+
+    def start_late(j):
         for way in range(2):
 
             @pl.when(late_columns[way])
             def _():
                 late(way, j).start()
 
+    def finish_late(j):
+        for way in range(2):
+
+            @pl.when(late_columns[way])
+            def _():
+                late(way, j).wait()
+                ring_in[way, part + j] = lax.select(late_wanted[way], late_in[way, j], ring_in[way, part + j])
+
+    def begin_last(j):
         for way in range(2):
 
             @pl.when(wraps[way])
             def _():
                 last_content(way, j)
-                hop(way, part + j).start()
+                if j >= EASY:
+                    hop(way, j).start()
 
     def finish_last(j):
-        for way in range(2):
-
-            @pl.when(late_columns[way])
-            def _():
-                late(way, j).wait()
-                ring_in[way, part + j] = lax.select(late_wanted[way], across[way, j], ring_in[way, part + j])
-
+        finish_late(j)
         for way in range(2):
 
             @pl.when(jnp.logical_not(wraps[way]))
@@ -332,8 +338,20 @@
     def ring_last(j):
         q = count + j
         for way in range(2):
-            hop(way, part + j).wait_recv()
-            ring_out[way, q] = lax.select(from_beside[way], across[way, part + j], passed[way, part + j])
+            if j >= EASY:
+                hop(way, j).wait_recv()
+                ring_out[way, q] = lax.select(from_beside[way], across[way, j], passed[way, j])
+            else:
+
+                @pl.when(wraps[way])
+                def _():
+                    ring_out[way, q] = passed[way, j]
+
+                @pl.when(jnp.logical_not(wraps[way]))
+                def _():
+                    hop(way, j).wait_recv()
+                    ring_out[way, q] = lax.select(from_beside[way], across[way, j], passed[way, j])
+
             ring(way, q).start()
 
     def passage_step(k, shares):
@@ -360,7 +378,9 @@
     landed(count - 1)
     ring_first(1)
     add_scores(count - 1)
-    swap = send(score_own, score_other, s_send, s_recv, me, 1 - core)
+    my_half = pl.ds(pl.multiple_of(core * half, half), half)
+    their_half = pl.ds(pl.multiple_of((1 - core) * half, half), half)
+    swap = send(score_own.at[their_half], score_other, s_send, s_recv, me, 1 - core)
     swap.start()
     ring_first(2)
     swap.wait_recv()
@@ -368,11 +388,12 @@
     scale = 3.0 / math.sqrt(2 * width)
 
     def soft_rows(group, total):
-        here = pl.ds(pl.multiple_of(group * GROUP, GROUP), GROUP)
+        here = pl.ds(pl.multiple_of(core * half + group * GROUP, GROUP), GROUP)
+        there = pl.ds(pl.multiple_of(group * GROUP, GROUP), GROUP)
         tiles = []
         for slot in range(NY):
             columns = slice(slot * rows, (slot + 1) * rows)
-            tile = (score_own[here, columns] + score_other[here, columns]) * scale
+            tile = (score_own[here, columns] + score_other[there, columns]) * scale
             if slot > 0:
                 tile = lax.select(linked[slot], tile, jnp.full_like(tile, -1e30))
             tiles.append(tile)
@@ -392,10 +413,7 @@
             coeff[slot, here, :] = value.astype(jnp.bfloat16)
         return total + heavy * (top + jnp.log(row_total) - picked)
 
-    total = lax.fori_loop(0, rows // GROUP, soft_rows, jnp.zeros((GROUP, 1), jnp.float32))
-    loss_tile[...] = jnp.broadcast_to(jnp.sum(total, axis=0, keepdims=True), loss_tile.shape)
-
-    my_half = pl.ds(pl.multiple_of(core * half, half), half)
+    total = lax.fori_loop(0, half // GROUP, soft_rows, jnp.zeros((GROUP, 1), jnp.float32))
     for s in range(1, NY):
         coeff_out[s - 1] = coeff[s, my_half, :]
     coeff_z = [
@@ -404,6 +422,12 @@
     ]
     for copy in coeff_z:
         copy.start()
+
+    halves = send(coeff.at[:, my_half, :], coeff.at[:, my_half, :], ch_send, ch_recv, me, 1 - core)
+    halves.start()
+    loss_core[core] = jnp.broadcast_to(jnp.sum(total, axis=0, keepdims=True), loss_tile.shape)
+    loss_across = send(loss_core.at[core], loss_core.at[core], lc_send, lc_recv.at[core], me, 1 - core)
+    loss_across.start()
 
     def spread(buffer, send_sem, recv_sem, mine_at, size, place):
         return [
@@ -421,14 +445,10 @@
             value = value + buffer[s]
         return value
 
-    loss_along_y = spread(loss_y, ly_send, ly_recv, y, NY, at_y)
-    for copy in loss_along_y:
-        copy.start()
-
     ring_first(3)
-    for j in range(2):
-        ring_landed(j)
-        pass_relayed(j)
+    ring_landed(0)
+    ring_landed(1)
+    halves.wait_recv()
 
     def query_grad_step(k, carry):
         value = nn_dot(coeff[0], own[k])
@@ -438,6 +458,14 @@
         return carry
 
     lax.fori_loop(0, count, query_grad_step, 0)
+
+    send(
+        loss_core.at[1 - core], loss_core.at[1 - core], lc_send, lc_recv.at[1 - core], me, 1 - core
+    ).wait_recv()
+    loss_tile[...] = loss_core[0] + loss_core[1]
+    loss_along_y = spread(loss_y, ly_send, ly_recv, y, NY, at_y)
+    for copy in loss_along_y:
+        copy.start()
 
     for copy in coeff_z:
         copy.wait_recv()
@@ -450,10 +478,12 @@
         send(coeff_staged.at[2], coeff_got.at[2], cy_send.at[1], cy_recv.at[1], at_y(2)),
         send(coeff_staged.at[3:5], coeff_got.at[0:2], cy_send.at[2], cy_recv.at[0], at_y(3)),
     ]
-    for copy in coeff_y:
-        copy.start()
+    for message in (0, 2, 1):
+        coeff_y[message].start()
 
     ring_second(0)
+    pass_relayed(0)
+    pass_relayed(1)
     ring_landed(2)
     pass_relayed(2)
     ring_second(1)
@@ -467,10 +497,14 @@
     for copy in loss_along_z:
         copy.start()
     ring_second(2)
-    for copy in coeff_y:
-        copy.wait_recv()
-    forward = send(coeff_got, coeff_fwd, cf_send, cf_recv, me, 1 - core)
-    forward.start()
+    coeff_y[0].wait_recv()
+    coeff_y[2].wait_recv()
+    forward = [
+        send(coeff_got.at[piece], coeff_fwd.at[piece], cf_send.at[i], cf_recv.at[i], me, 1 - core)
+        for i, piece in enumerate((slice(0, 2), slice(2, 3), slice(3, 5)))
+    ]
+    forward[0].start()
+    forward[2].start()
     ring_second(3)
 
     def turned(tile):
@@ -479,7 +513,10 @@
     coeff_t[0] = turned(coeff[0]).astype(jnp.bfloat16)
     middle_t[0] = turned(coeff[1]).astype(jnp.bfloat16)
     middle_t[1] = turned(coeff[3]).astype(jnp.bfloat16)
-    forward.wait_recv()
+    ring_landed(4)
+    start_late(0)
+    forward[0].wait_recv()
+    forward[2].wait_recv()
     first_half = core == 0
 
     def whole(place):
@@ -490,20 +527,25 @@
 
     middle_t[2] = whole(4).astype(jnp.bfloat16)
     middle_t[3] = whole(1).astype(jnp.bfloat16)
-    ring_landed(4)
     begin_last(0)
+    coeff_y[1].wait_recv()
+    forward[1].start()
+    ring_landed(5)
+    start_late(1)
+    begin_last(1)
+    finish_last(0)
+    ring_last(0)
+    forward[1].wait_recv()
     for slot, place in ((1, 0), (2, 2), (3, 3)):
         tile = whole(place)
         coeff_t[slot] = lax.select(linked[slot], tile, jnp.zeros_like(tile)).astype(jnp.bfloat16)
-    ring_landed(5)
-    begin_last(1)
-    finish_last(0)
-    ring_last(0)
     ring_landed(6)
+    start_late(2)
     begin_last(2)
     finish_last(1)
     ring_last(1)
     ring_landed(7)
+    start_late(3)
     begin_last(3)
     finish_last(2)
     ring_last(2)
@@ -535,15 +577,22 @@
         value = nn_dot(coeff_t[0], own[count + k]) + from_up + from_down + opposite
         passage_grad[:, k * CHUNK : (k + 1) * CHUNK] = value
 
-    for j in range(part):
+    for j in range(EASY):
         ring_landed(count + j)
+        start_late(part + j)
+    value = collect(loss_x, lx_recv, x, NX)
+    for copy in loss_along_x:
+        copy.wait_send()
+    loss_ref[...] = value * (1.0 / (rows * planes * NY))
+    for j in range(EASY, part):
+        ring_landed(count + j)
+        if j == EASY:
+            for i in range(EASY):
+                finish_late(part + i)
+                passage_grad_chunk(i, True)
+                passage_grad_chunk(part + i, False)
         passage_grad_chunk(j, True)
         passage_grad_chunk(part + j, False)
-        if j == 0:
-            value = collect(loss_x, lx_recv, x, NX)
-            for copy in loss_along_x:
-                copy.wait_send()
-            loss_ref[...] = value * (1.0 / (rows * planes * NY))
 
     def finish_shares(k, carry):
         for copy in along_z(k):
@@ -568,8 +617,15 @@
     lax.fori_loop(1, 2 * count, finish_shares, 0)
     lax.fori_loop(1, count, finish_chunks, 0)
     lax.fori_loop(0, count + part, finish_ring, 0)
-    lax.fori_loop(part, count, finish_hops, 0)
-    for copy in first_along_y() + first_along_z() + coeff_z + coeff_y + [swap, forward]:
+    for way in range(2):
+
+        @pl.when(jnp.logical_not(wraps[way]))
+        def _():
+            for j in range(EASY):
+                hop(way, j).wait_send()
+
+    lax.fori_loop(EASY, part, finish_hops, 0)
+    for copy in first_along_y() + first_along_z() + coeff_z + coeff_y + forward + [swap, halves, loss_across]:
         copy.wait_send()
 
 
@@ -592,12 +648,13 @@
         vmem((NY - 1, count, rows, CHUNK), low),
         vmem((NY - 1, rows, CHUNK), low),
         vmem((NY - 1, rows, CHUNK), low),
-        vmem((2, count, rows, CHUNK), low),
-        vmem((2, count, rows, CHUNK), low),
+        vmem((2, count // 2, rows, CHUNK), low),
+        vmem((2, count // 2, rows, CHUNK), low),
         vmem((2, slots, rows, CHUNK), low),
         vmem((2, slots, rows, CHUNK), low),
+        vmem((2, count // 2 + EASY, rows, CHUNK), low),
         vmem((rows, NY * rows), full),
-        vmem((rows, NY * rows), full),
+        vmem((rows // 2, NY * rows), full),
         vmem((NY, rows, rows), low),
         vmem((NY - 1, rows // 2, rows), low),
         vmem((NY - 1, rows // 2, rows), low),
@@ -609,6 +666,7 @@
         vmem((rows, 128), full),
         vmem((rows, 128), full),
         vmem(tile, full),
+        vmem((2,) + tile, full),
         vmem((NY,) + tile, full),
         vmem((NZ,) + tile, full),
         vmem((NX,) + tile, full),
@@ -620,14 +678,17 @@
         dma, dma,
         dma((NY - 1,)), dma((NY - 1,)),
         dma((NY - 1,)), dma((NY - 1,)),
-        dma, dma,
+        dma((3,)), dma((3,)),
         dma((NY,)), dma((NY,)),
         dma((NZ,)), dma((NZ,)),
         dma((NX,)), dma((NX,)),
         dma((NY - 1,)), dma((NY - 1,)),
         dma((3,)),
         dma((2, slots)), dma((2, slots)),
-        dma((2, count)), dma((2, count)),
+        dma((2, count // 2)), dma((2, count // 2)),
+        dma((2, count // 2 + EASY)), dma((2, count // 2 + EASY)),
+        dma, dma,
+        dma, dma((2,)),
     ]
     in_vmem = pl.BlockSpec(memory_space=pltpu.VMEM)
     loss, query_grad, passage_grad = pl.pallas_call(

time: 109 us -> 105 us (0.963)
  Pallas kernels: 105 us -> 101 us
    pallas_call x1, Pallas kernels: 105 us -> 101 us  [shards(): pl.pallas_call(kernel, out_shape=[jax.ShapeDtypeStruct(tile, full), vmem(...]
where the time goes in v6:
time: 105 us
  Pallas kernels  101 us (96%)
  local copies, waits for them, and re-layouts  3.15 us (3%)
    pallas_call x1, Pallas kernels, shards(): pl.pallas_call(kernel, out_shape=[jax.ShapeDtypeStruct(tile, full), vmem(...  101 us
    unnamed x2, local copies, waits for them, and re-layouts  2.64 us

profile of v6, /device:TPU:1, one launch (start us, length us, event | category | flops | bytes accessed | tf_op | source)
XLA Modules:
  0.0 105.0 jit_solution(2735861329237398189)
XLA Ops:
  0.6 101.2 %shard_map.76 = (f32[8,128]{1,0:T(8,128)S(1)}, f32[256,2048]{1,0:T(8,128)S(1)}, f32[256,2048]{1,0:T(8,128)S(1)}) custom-call(f32[256,2048]{1,0:T(8,128)} %query_hbm.1, f32[256,2048]{1,0:T(8,128)} %passage_hbm.1, s32[128]{0:T(128)} %cluster_hbm.1, s32[2,128]{1,0:T(2,128)} %bitcast.3, f32[2,128]{1,0:T(2,128)} %bitcast.4), custom_call_target="tpu_custom_call" | custom-call | flops 3221225472 | bytes 8388608 | tf_op jit(solution)/shard_map/pallas_call | solution.py:694
  101.8 0.5 slice.3
  102.3 1.3 %copy.10 = f32[256,2048]{1,0:T(8,128)} copy(f32[256,2048]{1,0:T(8,128)S(1)} %get-tuple-element.10) | data formatting | bytes 4194304
  103.6 1.3 %copy.11 = f32[256,2048]{1,0:T(8,128)} copy(f32[256,2048]{1,0:T(8,128)S(1)} %get-tuple-element.11) | data formatting | bytes 4194304

commit v7 on v6

--- a/solution.py
+++ b/solution.py
@@ -96,8 +96,6 @@
     for peer in peers:
         pl.semaphore_signal(barrier, inc=1, device_id=(peer, core), device_id_type=MESH)
     pl.semaphore_signal(barrier, inc=1, device_id=(me, 1 - core), device_id_type=MESH)
-    pl.semaphore_wait(barrier, len(peers) + 1)
-
     for copy in small:
         copy.wait()
 
@@ -205,6 +203,7 @@
         ]
 
     cast_passage(0)
+    pl.semaphore_wait(barrier, len(peers) + 1)
     for copy in first_along_y():
         copy.start()
     for k in range(1, 4):
@@ -584,7 +583,7 @@
     for copy in loss_along_x:
         copy.wait_send()
     loss_ref[...] = value * (1.0 / (rows * planes * NY))
-    for j in range(EASY, part):
+    for j in range(EASY, part - 1):
         ring_landed(count + j)
         if j == EASY:
             for i in range(EASY):
@@ -616,7 +615,7 @@
 
     lax.fori_loop(1, 2 * count, finish_shares, 0)
     lax.fori_loop(1, count, finish_chunks, 0)
-    lax.fori_loop(0, count + part, finish_ring, 0)
+    lax.fori_loop(0, count + part - 2, finish_ring, 0)
     for way in range(2):
 
         @pl.when(jnp.logical_not(wraps[way]))
@@ -627,6 +626,45 @@
     lax.fori_loop(EASY, part, finish_hops, 0)
     for copy in first_along_y() + first_along_z() + coeff_z + coeff_y + forward + [swap, halves, loss_across]:
         copy.wait_send()
+
+    ring_landed(count + part - 1)
+    passage_grad_chunk(part - 1, True)
+    passage_grad_chunk(count - 1, False)
+    lax.fori_loop(count + part - 2, count + part, finish_ring, 0)
+
+
+PIECES = 4
+
+
+def write_kernel(loss, query_grad, passage_grad, loss_ref, query_grad_hbm, passage_grad_hbm, sem):
+    loss_ref[...] = loss[0:1, 0:1]
+    size = query_grad.shape[0] // PIECES
+    copies = []
+    for i, (source, target) in enumerate([(query_grad, query_grad_hbm), (passage_grad, passage_grad_hbm)]):
+        for piece in range(PIECES):
+            here = pl.ds(piece * size, size)
+            copies.append(pltpu.make_async_copy(source.at[here], target.at[here], sem.at[i, piece]))
+    for copy in copies:
+        copy.start()
+    for copy in copies:
+        copy.wait()
+
+
+def write_out(loss, query_grad, passage_grad):
+    vmem, anywhere = pl.BlockSpec(memory_space=pltpu.VMEM), pl.BlockSpec(memory_space=pltpu.HBM)
+    loss, query_grad, passage_grad = pl.pallas_call(
+        write_kernel,
+        out_shape=[
+            jax.ShapeDtypeStruct((1, 1), jnp.float32),
+            jax.ShapeDtypeStruct(query_grad.shape, jnp.float32),
+            jax.ShapeDtypeStruct(passage_grad.shape, jnp.float32),
+        ],
+        in_specs=[vmem, vmem, vmem],
+        out_specs=[vmem, anywhere, anywhere],
+        scratch_shapes=[pltpu.SemaphoreType.DMA((2, PIECES))],
+        compiler_params=pltpu.CompilerParams(vmem_limit_bytes=2**20),
+    )(*[pltpu.with_memory_space_constraint(a, pltpu.VMEM) for a in (loss, query_grad, passage_grad)])
+    return loss[0, 0], query_grad, passage_grad
 
 
 def shards(queries, passages, cluster_of_block, positive_row, query_weight):
@@ -702,7 +740,7 @@
         out_specs=[in_vmem, in_vmem, in_vmem],
         scratch_shapes=scratch,
         compiler_params=pltpu.CompilerParams(
-            collective_id=0, has_side_effects=True, vmem_limit_bytes=48 * 2**20
+            collective_id=0, has_side_effects=True, vmem_limit_bytes=36 * 2**20
         ),
         cost_estimate=pl.CostEstimate(
             flops=6 * NY * rows * rows * width, bytes_accessed=16 * rows * width, transcendentals=NY * rows * rows
@@ -716,7 +754,7 @@
             )
         ]
     )
-    return loss[0, 0], query_grad, passage_grad
+    return write_out(loss, query_grad, passage_grad)
 
 
 def solution(mesh):

time: 105 us -> 105 us (level)
  local copies, waits for them, and re-layouts: 3.15 us -> 0 us
  Pallas kernels: 101 us -> 103 us
    unnamed x2 -> x0, local copies, waits for them, and re-layouts: 2.64 us -> none
    pallas_call x0 -> x1, Pallas kernels: none -> 2.58 us  [write_out(): pl.pallas_call(write_kernel, out_shape=[jax.ShapeDtypeStruct((1, 1), jnp....]
where the time goes in v7:
time: 105 us; the launch traced here: 104 us
  Pallas kernels  103 us (98%)
    pallas_call x1, Pallas kernels, shards(): pl.pallas_call(kernel, out_shape=[jax.ShapeDtypeStruct(tile, full), vmem(...  101 us
    pallas_call x1, Pallas kernels, write_out(): pl.pallas_call(write_kernel, out_shape=[jax.ShapeDtypeStruct((1, 1), jnp....  2.58 us

profile of v7, /device:TPU:1, one launch (start us, length us, event | category | flops | bytes accessed | tf_op | source)
XLA Modules:
  0.0 104.0 jit_solution(7907982841727874496)
XLA Ops:
  0.6 100.8 %shard_map.76 = (f32[8,128]{1,0:T(8,128)S(1)}, f32[256,2048]{1,0:T(8,128)S(1)}, f32[256,2048]{1,0:T(8,128)S(1)}) custom-call(f32[256,2048]{1,0:T(8,128)} %query_hbm.1, f32[256,2048]{1,0:T(8,128)} %passage_hbm.1, s32[128]{0:T(128)} %cluster_hbm.1, s32[2,128]{1,0:T(2,128)} %bitcast.3, f32[2,128]{1,0:T(2,128)} %bitcast.4), custom_call_target="tpu_custom_call" | custom-call | flops 3221225472 | bytes 8388608 | tf_op jit(solution)/shard_map/pallas_call | solution.py:732
  101.4 2.6 %shard_map.77 = (f32[1,1]{1,0:T(1,128)}, f32[256,2048]{1,0:T(8,128)}, f32[256,2048]{1,0:T(8,128)}) custom-call(f32[8,128]{1,0:T(8,128)S(1)} %get-tuple-element.9.loss, f32[256,2048]{1,0:T(8,128)S(1)} %get-tuple-element.10.query_grad, f32[256,2048]{1,0:T(8,128)S(1)} %get-tuple-element.11.passage_grad), custom_call_target="tpu_custom_call" | custom-call | tf_op jit(solution)/shard_map/pallas_call | solution.py:655

commit v8 on v7

--- a/solution.py
+++ b/solution.py
@@ -456,7 +456,6 @@
         query_grad[:, pl.ds(pl.multiple_of(k * CHUNK, CHUNK), CHUNK)] = value
         return carry
 
-    lax.fori_loop(0, count, query_grad_step, 0)
 
     send(
         loss_core.at[1 - core], loss_core.at[1 - core], lc_send, lc_recv.at[1 - core], me, 1 - core
@@ -486,6 +485,7 @@
     ring_landed(2)
     pass_relayed(2)
     ring_second(1)
+    lax.fori_loop(0, count, query_grad_step, 0)
     ring_landed(3)
     pass_relayed(3)
     value = collect(loss_y, ly_recv, y, NY)

time: 105 us -> 105 us (level)
  no operation moved by 1% of the time
where the time goes in v8:
time: 105 us; the launch traced here: 104 us
  Pallas kernels  104 us (99%)
    pallas_call x1, Pallas kernels, shards(): pl.pallas_call(kernel, out_shape=[jax.ShapeDtypeStruct(tile, full), vmem(...  101 us
    pallas_call x1, Pallas kernels, write_out(): pl.pallas_call(write_kernel, out_shape=[jax.ShapeDtypeStruct((1, 1), jnp....  2.58 us

profile of v8, /device:TPU:1, one launch (start us, length us, event | category | flops | bytes accessed | tf_op | source)
XLA Modules:
  0.0 104.2 jit_solution(9876877056024211096)
XLA Ops:
  0.6 101.0 %shard_map.76 = (f32[8,128]{1,0:T(8,128)S(1)}, f32[256,2048]{1,0:T(8,128)S(1)}, f32[256,2048]{1,0:T(8,128)S(1)}) custom-call(f32[256,2048]{1,0:T(8,128)} %query_hbm.1, f32[256,2048]{1,0:T(8,128)} %passage_hbm.1, s32[128]{0:T(128)} %cluster_hbm.1, s32[2,128]{1,0:T(2,128)} %bitcast.3, f32[2,128]{1,0:T(2,128)} %bitcast.4), custom_call_target="tpu_custom_call" | custom-call | flops 3221225472 | bytes 8388608 | tf_op jit(solution)/shard_map/pallas_call | solution.py:732
  101.6 2.6 %shard_map.77 = (f32[1,1]{1,0:T(1,128)}, f32[256,2048]{1,0:T(8,128)}, f32[256,2048]{1,0:T(8,128)}) custom-call(f32[8,128]{1,0:T(8,128)S(1)} %get-tuple-element.9.loss, f32[256,2048]{1,0:T(8,128)S(1)} %get-tuple-element.10.query_grad, f32[256,2048]{1,0:T(8,128)S(1)} %get-tuple-element.11.passage_grad), custom_call_target="tpu_custom_call" | custom-call | tf_op jit(solution)/shard_map/pallas_call | solution.py:655
